TPU v7x, 128 devices: a whole 4x4x4 slice. The times are simulated.
128 devices in a mesh: section: 2 (over core), seq: 4 (over x), wa: 16 (over z, y).
Axes of the slice: x: 4, y: 4, z: 4, core: 2. Of those that a mesh axis runs over, the one named last changes fastest.
Arguments:
- tokens: bfloat16 [4, 1024, 1024], P(None, 'seq'), may hold values from -6 to 6
- cotangent: float32 [4, 1024, 1024], P(None, 'seq'), may hold values from -6 to 6
- in_weight: bfloat16 [2, 1024, 3, 1024], P('section', None, None, 'wa'), may hold values from -0.1875 to 0.1875
- conv_weight: float32 [2, 3, 1024], P('section', None, 'wa'), may hold values from -3 to 3
- out_weight: bfloat16 [2, 1024, 1024], P('section', 'wa'), may hold values from -0.1875 to 0.1875
- norm_gain: float32 [2, 1024], P('section'), may hold values from 0.25 to 1.75
- gate_up_weight: bfloat16 [2, 1024, 2, 4608], P('section', None, None, 'wa'), may hold values from -0.1875 to 0.1875
- down_weight: bfloat16 [2, 4608, 1024], P('section', 'wa'), may hold values from -0.09375 to 0.09375
Outputs:
- layer_out: bfloat16 [2, 4, 1024, 1024], P('section', None, ('seq', 'wa'))
- input_grad: float32 [2, 4, 1024, 1024], P('section', None, ('seq', 'wa'))
- in_weight_grad: float32 [2, 1024, 3, 1024], P('section', None, None, 'wa')
- conv_weight_grad: float32 [2, 3, 1024], P('section', None, 'wa')
- out_weight_grad: float32 [2, 1024, 1024], P('section', 'wa')
- norm_gain_grad: float32 [2, 1024], P('section')
- gate_up_grad: float32 [2, 1024, 2, 4608], P('section', None, None, 'wa')
- down_grad: float32 [2, 4608, 1024], P('section', 'wa')
All inputs are finite; a program needn't handle non-finite values.
Results may differ from a plain program's by a relative error of at most 0.025.
Values may be sent and summed in bfloat16 or wider, within the bound.
A program may use at most 128 MiB of HBM per device.

v0:
```python
import jax
import jax.numpy as jnp
from jax import lax
from jax.sharding import PartitionSpec as P

EPSILON = 1e-05


def passed_along(block, axis, distance):
    devices = range(lax.axis_size(axis))
    route = [((i - distance) % len(devices), i) for i in devices]
    return lax.ppermute(block, axis, route)


def shifted(block, axis, distance):
    devices = range(lax.axis_size(axis))
    route = [(i - distance, i) for i in devices if i - distance in devices]
    return lax.ppermute(block, axis, route)


def contract_first(lhs_matrix, rhs_matrix):
    return lax.dot_general(
        lhs_matrix, rhs_matrix, (((0,), (0,)), ((), ())), preferred_element_type=jnp.float32
    )


def contract_last(lhs_matrix, rhs_matrix):
    return lax.dot_general(
        lhs_matrix, rhs_matrix, (((1,), (1,)), ((), ())), preferred_element_type=jnp.float32
    )


def silu_parts(gate_val):
    sigmoid_val = jax.nn.sigmoid(gate_val)
    return (gate_val * sigmoid_val, sigmoid_val * (1.0 + gate_val * (1.0 - sigmoid_val)))


def body(
    tokens, cotangent, in_weight, conv_weight, out_weight, norm_gain, gate_up_weight, down_weight
):
    micro_count, block_rows, model_width = tokens.shape
    section_index = lax.axis_index("section")
    seq_index = lax.axis_index("seq")
    seq_count = lax.axis_size("seq")
    wa_index = lax.axis_index("wa")
    share_rows = block_rows // lax.axis_size("wa")
    share_start = wa_index * share_rows
    local_width = conv_weight.shape[2]
    hidden_width = gate_up_weight.shape[3]
    in_matrix = in_weight[0].reshape(model_width, 3 * local_width)
    conv_taps = conv_weight[0]
    out_matrix = out_weight[0]
    gain_row = norm_gain[0]
    gate_up = gate_up_weight[0].reshape(model_width, 2 * hidden_width)
    down_matrix = down_weight[0]
    edge_zeros = jnp.zeros((2, local_width), jnp.bfloat16)
    received = jnp.zeros((block_rows, model_width), jnp.bfloat16)
    carried = edge_zeros
    outputs = []
    saved = []
    for step_num in range(micro_count + 1):
        micro_index = step_num - section_index
        inputs = jnp.where(section_index == 0, tokens[min(step_num, micro_count - 1)], received)
        projected = jnp.dot(inputs, in_matrix, preferred_element_type=jnp.float32).reshape(
            block_rows, 3, local_width
        )
        gated_in = (projected[:, 0] * projected[:, 2]).astype(jnp.bfloat16)
        incoming = passed_along(gated_in[block_rows - 2 :], "seq", 1)
        first_rows = jnp.where(
            seq_index == 0, jnp.where(micro_index == 0, edge_zeros, carried), incoming
        )
        carried = incoming
        padded = jnp.concatenate([first_rows, gated_in], 0).astype(jnp.float32)
        conv_out = (
            conv_taps[0] * padded[:block_rows]
            + conv_taps[1] * padded[1 : block_rows + 1]
            + conv_taps[2] * padded[2:]
        )
        mixed_in = (projected[:, 1] * conv_out).astype(jnp.bfloat16)
        mixed_sum = lax.psum(
            jnp.dot(mixed_in, out_matrix, preferred_element_type=jnp.float32), "wa"
        )
        residual = inputs.astype(jnp.float32) + mixed_sum
        inv_rms = lax.rsqrt(jnp.mean(residual * residual, -1, keepdims=True) + EPSILON)
        normed = (residual * inv_rms * gain_row).astype(jnp.bfloat16)
        gate_up_val = jnp.dot(normed, gate_up, preferred_element_type=jnp.float32).reshape(
            block_rows, 2, hidden_width
        )
        gate_val = gate_up_val[:, 0]
        up_val = gate_up_val[:, 1]
        hidden = (silu_parts(gate_val)[0] * up_val).astype(jnp.bfloat16)
        own_residual = lax.dynamic_slice_in_dim(residual, share_start, share_rows, 0)
        layer_rows = (
            own_residual
            + lax.psum_scatter(
                jnp.dot(hidden, down_matrix, preferred_element_type=jnp.float32),
                "wa",
                scatter_dimension=0,
                tiled=True,
            )
        ).astype(jnp.bfloat16)
        outputs.append(layer_rows)
        saved.append(
            (
                inputs,
                projected,
                padded,
                conv_out,
                mixed_in,
                residual,
                inv_rms,
                normed,
                gate_val,
                up_val,
                hidden,
            )
        )
        if step_num < micro_count:
            arrived = shifted(layer_rows, "section", 1)
            received = lax.all_gather(arrived, "wa", axis=0, tiled=True)
    stacked_out = jnp.stack(outputs)
    layer_block = jnp.where(section_index == 0, stacked_out[:micro_count], stacked_out[1:])
    tail_zeros = jnp.zeros((2, local_width), jnp.float32)
    received_grad = jnp.zeros((block_rows, model_width), jnp.float32)
    carried_grad = tail_zeros
    in_total = jnp.zeros((model_width, 3 * local_width), jnp.float32)
    tap_total = jnp.zeros((3, local_width), jnp.float32)
    out_total = jnp.zeros((local_width, model_width), jnp.float32)
    gain_total = jnp.zeros((model_width,), jnp.float32)
    gate_up_total = jnp.zeros((model_width, 2 * hidden_width), jnp.float32)
    down_total = jnp.zeros((hidden_width, model_width), jnp.float32)
    grad_rows = []
    for step_num in range(micro_count + 1):
        micro_index = micro_count - 1 - step_num + (1 - section_index)
        valid = (micro_index >= 0) & (micro_index < micro_count)
        (
            inputs,
            projected,
            padded,
            conv_out,
            mixed_in,
            residual,
            inv_rms,
            normed,
            gate_val,
            up_val,
            hidden,
        ) = saved[micro_count - step_num]
        out_grad = jnp.where(
            section_index == 1, cotangent[max(micro_count - 1 - step_num, 0)], received_grad
        )
        out_bf = out_grad.astype(jnp.bfloat16)
        hidden_grad = contract_last(out_bf, down_matrix)
        silu_val, silu_slope = silu_parts(gate_val)
        gate_up_bf = (
            jnp.stack([hidden_grad * up_val * silu_slope, hidden_grad * silu_val], 1)
            .astype(jnp.bfloat16)
            .reshape(block_rows, 2 * hidden_width)
        )
        normed_grad = lax.psum(
            contract_last(gate_up_bf, gate_up).astype(jnp.bfloat16), "wa"
        ).astype(jnp.float32)
        scaled_grad = normed_grad * gain_row
        gain_term = jnp.sum(normed_grad * residual * inv_rms, 0)
        residual_grad = (
            out_grad
            + inv_rms * scaled_grad
            - residual * inv_rms**3 * jnp.mean(scaled_grad * residual, -1, keepdims=True)
        )
        residual_bf = residual_grad.astype(jnp.bfloat16)
        mixed_grad = contract_last(residual_bf, out_matrix)
        c_grad = mixed_grad * conv_out
        conv_grad = mixed_grad * projected[:, 1]
        incoming_grad = passed_along(conv_grad[:2], "seq", -1)
        last_rows = jnp.where(
            seq_index == seq_count - 1,
            jnp.where(micro_index == micro_count - 1, tail_zeros, carried_grad),
            incoming_grad,
        )
        carried_grad = incoming_grad
        extended = jnp.concatenate([conv_grad, last_rows], 0)
        gated_grad = (
            conv_taps[2] * extended[:block_rows]
            + conv_taps[1] * extended[1 : block_rows + 1]
            + conv_taps[0] * extended[2:]
        )
        tap_grad = jnp.stack(
            [jnp.sum(conv_grad * padded[offset : offset + block_rows], 0) for offset in range(3)]
        )
        proj_bf = (
            jnp.stack([gated_grad * projected[:, 2], c_grad, gated_grad * projected[:, 0]], 1)
            .astype(jnp.bfloat16)
            .reshape(block_rows, 3 * local_width)
        )
        own_grad = lax.dynamic_slice_in_dim(residual_grad, share_start, share_rows, 0)
        input_rows_grad = own_grad + lax.psum_scatter(
            contract_last(proj_bf, in_matrix).astype(jnp.bfloat16),
            "wa",
            scatter_dimension=0,
            tiled=True,
        ).astype(jnp.float32)
        grad_rows.append(input_rows_grad)
        in_total = in_total + jnp.where(valid, contract_first(inputs, proj_bf), 0.0)
        tap_total = tap_total + jnp.where(valid, tap_grad, 0.0)
        out_total = out_total + jnp.where(valid, contract_first(mixed_in, residual_bf), 0.0)
        gain_total = gain_total + jnp.where(valid, gain_term, 0.0)
        gate_up_total = gate_up_total + jnp.where(valid, contract_first(normed, gate_up_bf), 0.0)
        down_total = down_total + jnp.where(valid, contract_first(hidden, out_bf), 0.0)
        if step_num < micro_count:
            arrived_grad = shifted(input_rows_grad.astype(jnp.bfloat16), "section", -1).astype(
                input_rows_grad.dtype
            )
            received_grad = lax.all_gather(
                arrived_grad.astype(jnp.bfloat16), "wa", axis=0, tiled=True
            ).astype(arrived_grad.dtype)
    stacked_grad = jnp.stack(grad_rows)
    grad_block = jnp.where(section_index == 1, stacked_grad[:micro_count], stacked_grad[1:])[::-1]
    in_sum, tap_sum, out_sum, gain_sum, gate_up_sum, down_sum = (
        lax.psum(in_total.astype(jnp.bfloat16), "seq").astype(jnp.float32),
        lax.psum(tap_total.astype(jnp.bfloat16), "seq").astype(jnp.float32),
        lax.psum(out_total.astype(jnp.bfloat16), "seq").astype(jnp.float32),
        lax.psum(gain_total.astype(jnp.bfloat16), "seq").astype(jnp.float32),
        lax.psum(gate_up_total.astype(jnp.bfloat16), "seq").astype(jnp.float32),
        lax.psum(down_total.astype(jnp.bfloat16), "seq").astype(jnp.float32),
    )
    return (
        layer_block[None],
        grad_block[None],
        in_sum.reshape(1, model_width, 3, local_width),
        tap_sum[None],
        out_sum[None],
        gain_sum[None],
        gate_up_sum.reshape(1, model_width, 2, hidden_width),
        down_sum[None],
    )


def solution(mesh):
    in_specs = (
        P(None, "seq", None),
        P(None, "seq", None),
        P("section", None, None, "wa"),
        P("section", None, "wa"),
        P("section", "wa", None),
        P("section", None),
        P("section", None, None, "wa"),
        P("section", "wa", None),
    )
    out_specs = (
        P("section", None, ("seq", "wa"), None),
        P("section", None, ("seq", "wa"), None),
        P("section", None, None, "wa"),
        P("section", None, "wa"),
        P("section", "wa", None),
        P("section", None),
        P("section", None, None, "wa"),
        P("section", "wa", None),
    )
    return jax.shard_map(body, mesh=mesh, in_specs=in_specs, out_specs=out_specs, check_vma=False)
```

profile of v0, /device:TPU:0, one launch (start us, length us, event | category | flops | bytes accessed | tf_op | source)
XLA Modules:
  0.0 2036.5 jit_solution(783066171614633669)
XLA Ops:
  10.5 3.4 collective-permute-done
  16.8 88.5 %all-reduce.14.cloned.1.call-done = f32[256,1024]{1,0:T(8,128)} async-done(((f32[256,1024]{1,0:T(8,128)}), f32[256,1024]{1,0:T(8,128)}) %all-reduce.14.cloned.1.call-update) | async-done | bytes 1048592 | tf_op jit(solution)/shard_map/psum | solution.py:80
  110.1 72.3 %reduce-scatter.11.cloned.1.call-done = f32[16,1024]{1,0:T(8,128)} async-done(((f32[256,1024]{1,0:T(8,128)}), f32[16,1024]{1,0:T(8,128)}) %reduce-scatter.11.cloned.1.call-update) | async-done | bytes 65552 | tf_op jit(solution)/shard_map/reduce_scatter | solution.py:95
  185.4 23.3 %all_gather.24 = bf16[256,1024]{1,0:T(8,128)(2,1)S(1)} all-gather(bf16[16,1024]{1,0:T(8,128)(2,1)S(1)} %collective-permute-done.1), channel_id=1, replica_groups=mesh['section'=2,'seq'=4,'wa'=16] {'wa'}, dimensions={0}, use_global_device_ids=true | all-gather | bytes 557056 | tf_op jit(solution)/shard_map/all_gather | solution.py:120
  211.7 3.5 collective-permute-done.2
  218.0 84.7 %all-reduce.16.cloned.1.call-done = f32[256,1024]{1,0:T(8,128)} async-done(((f32[256,1024]{1,0:T(8,128)}), f32[256,1024]{1,0:T(8,128)}) %all-reduce.16.cloned.1.call-update) | async-done | bytes 1048592 | tf_op jit(solution)/shard_map/psum | solution.py:80
  307.7 72.3 %reduce-scatter.13.cloned.1.call-done = f32[16,1024]{1,0:T(8,128)} async-done(((f32[256,1024]{1,0:T(8,128)}), f32[16,1024]{1,0:T(8,128)}) %reduce-scatter.13.cloned.1.call-update) | async-done | bytes 65552 | tf_op jit(solution)/shard_map/reduce_scatter | solution.py:95
  383.0 23.3 %all_gather.25 = bf16[256,1024]{1,0:T(8,128)(2,1)S(1)} all-gather(bf16[16,1024]{1,0:T(8,128)(2,1)S(1)} %collective-permute-done.3), channel_id=1, replica_groups=mesh['section'=2,'seq'=4,'wa'=16] {'wa'}, dimensions={0}, use_global_device_ids=true | all-gather | bytes 557056 | tf_op jit(solution)/shard_map/all_gather | solution.py:120
  412.0 3.8 collective-permute-done.4
  421.6 84.6 %all-reduce.18.cloned.1.call-done = f32[256,1024]{1,0:T(8,128)} async-done(((f32[256,1024]{1,0:T(8,128)}), f32[256,1024]{1,0:T(8,128)}) %all-reduce.18.cloned.1.call-update) | async-done | bytes 1048592 | tf_op jit(solution)/shard_map/psum | solution.py:80
  511.4 72.3 %reduce-scatter.15.cloned.1.call-done = f32[16,1024]{1,0:T(8,128)} async-done(((f32[256,1024]{1,0:T(8,128)}), f32[16,1024]{1,0:T(8,128)}) %reduce-scatter.15.cloned.1.call-update) | async-done | bytes 65552 | tf_op jit(solution)/shard_map/reduce_scatter | solution.py:95
  586.7 23.3 %all_gather.26 = bf16[256,1024]{1,0:T(8,128)(2,1)S(1)} all-gather(bf16[16,1024]{1,0:T(8,128)(2,1)S(1)} %collective-permute-done.5), channel_id=1, replica_groups=mesh['section'=2,'seq'=4,'wa'=16] {'wa'}, dimensions={0}, use_global_device_ids=true | all-gather | bytes 557056 | tf_op jit(solution)/shard_map/all_gather | solution.py:120
  615.8 3.8 collective-permute-done.6
  625.3 84.7 %all-reduce.20.cloned.1.call-done = f32[256,1024]{1,0:T(8,128)} async-done(((f32[256,1024]{1,0:T(8,128)}), f32[256,1024]{1,0:T(8,128)}) %all-reduce.20.cloned.1.call-update) | async-done | bytes 1048592 | tf_op jit(solution)/shard_map/psum | solution.py:80
  715.2 72.3 %reduce-scatter.17.cloned.1.call-done = f32[16,1024]{1,0:T(8,128)} async-done(((f32[256,1024]{1,0:T(8,128)}), f32[16,1024]{1,0:T(8,128)}) %reduce-scatter.17.cloned.1.call-update) | async-done | bytes 65552 | tf_op jit(solution)/shard_map/reduce_scatter | solution.py:95
  790.6 23.3 %all_gather.27 = bf16[256,1024]{1,0:T(8,128)(2,1)S(1)} all-gather(bf16[16,1024]{1,0:T(8,128)(2,1)S(1)} %collective-permute-done.7), channel_id=1, replica_groups=mesh['section'=2,'seq'=4,'wa'=16] {'wa'}, dimensions={0}, use_global_device_ids=true | all-gather | bytes 557056 | tf_op jit(solution)/shard_map/all_gather | solution.py:120
  819.6 3.8 collective-permute-done.8
  829.3 84.5 %all-reduce.22.cloned.1.call-done = f32[256,1024]{1,0:T(8,128)} async-done(((f32[256,1024]{1,0:T(8,128)}), f32[256,1024]{1,0:T(8,128)}) %all-reduce.22.cloned.1.call-update) | async-done | bytes 1048592 | tf_op jit(solution)/shard_map/psum | solution.py:80
  917.7 1.8 fusion.147
  921.7 84.6 %all-reduce.24.cloned.1.call-done = bf16[256,1024]{1,0:T(8,128)(2,1)} async-done(((bf16[256,1024]{1,0:T(8,128)(2,1)}), bf16[256,1024]{1,0:T(8,128)(2,1)}) %all-reduce.24.cloned.1.call-update) | async-done | bytes 524304 | tf_op jit(solution)/shard_map/psum | solution.py:160
  1006.3 2.4 fusion.53
  1011.4 2.7 collective-permute-start.9
  1017.7 72.3 %reduce-scatter.21.cloned.1.call-done = bf16[16,1024]{1,0:T(8,128)(2,1)} async-done(((bf16[256,1024]{1,0:T(8,128)(2,1)}), bf16[16,1024]{1,0:T(8,128)(2,1)}) %reduce-scatter.21.cloned.1.call-update) | async-done | bytes 32784 | tf_op jit(solution)/shard_map/reduce_scatter | solution.py:196
  1092.8 1.8 collective-permute-done.10
  1094.6 23.3 %all_gather.28 = bf16[256,1024]{1,0:T(8,128)(2,1)S(1)} all-gather(bf16[16,1024]{1,0:T(8,128)(2,1)S(1)} %collective-permute-done.10), channel_id=1, replica_groups=mesh['section'=2,'seq'=4,'wa'=16] {'wa'}, dimensions={0}, use_global_device_ids=true | all-gather | bytes 557056 | tf_op jit(solution)/shard_map/all_gather | solution.py:213
  1117.9 2.1 fusion.139
  1122.2 84.0 %all-reduce.26.cloned.1.call-done = bf16[256,1024]{1,0:T(8,128)(2,1)} async-done(((bf16[256,1024]{1,0:T(8,128)(2,1)}), bf16[256,1024]{1,0:T(8,128)(2,1)}) %all-reduce.26.cloned.1.call-update) | async-done | bytes 524304 | tf_op jit(solution)/shard_map/psum | solution.py:160
  1206.2 2.4 fusion.55
  1208.7 1.8 fusion.47
  1211.5 2.7 collective-permute-start.11
  1217.8 72.3 %reduce-scatter.23.cloned.1.call-done = bf16[16,1024]{1,0:T(8,128)(2,1)} async-done(((bf16[256,1024]{1,0:T(8,128)(2,1)}), bf16[16,1024]{1,0:T(8,128)(2,1)}) %reduce-scatter.23.cloned.1.call-update) | async-done | bytes 32784 | tf_op jit(solution)/shard_map/reduce_scatter | solution.py:196
  1293.0 1.8 collective-permute-done.12
  1294.8 23.3 %all_gather.29 = bf16[256,1024]{1,0:T(8,128)(2,1)S(1)} all-gather(bf16[16,1024]{1,0:T(8,128)(2,1)S(1)} %collective-permute-done.12), channel_id=1, replica_groups=mesh['section'=2,'seq'=4,'wa'=16] {'wa'}, dimensions={0}, use_global_device_ids=true | all-gather | bytes 557056 | tf_op jit(solution)/shard_map/all_gather | solution.py:213
  1318.1 2.1 fusion.131
  1322.4 84.0 %all-reduce.28.cloned.1.call-done = bf16[256,1024]{1,0:T(8,128)(2,1)} async-done(((bf16[256,1024]{1,0:T(8,128)(2,1)}), bf16[256,1024]{1,0:T(8,128)(2,1)}) %all-reduce.28.cloned.1.call-update) | async-done | bytes 524304 | tf_op jit(solution)/shard_map/psum | solution.py:160
  1406.4 2.4 fusion.57
  1408.9 1.8 fusion.44
  1411.6 2.7 collective-permute-start.13
  1418.0 72.3 %reduce-scatter.25.cloned.1.call-done = bf16[16,1024]{1,0:T(8,128)(2,1)} async-done(((bf16[256,1024]{1,0:T(8,128)(2,1)}), bf16[16,1024]{1,0:T(8,128)(2,1)}) %reduce-scatter.25.cloned.1.call-update) | async-done | bytes 32784 | tf_op jit(solution)/shard_map/reduce_scatter | solution.py:196
  1493.1 1.8 collective-permute-done.14
  1494.9 23.3 %all_gather.30 = bf16[256,1024]{1,0:T(8,128)(2,1)S(1)} all-gather(bf16[16,1024]{1,0:T(8,128)(2,1)S(1)} %collective-permute-done.14), channel_id=1, replica_groups=mesh['section'=2,'seq'=4,'wa'=16] {'wa'}, dimensions={0}, use_global_device_ids=true | all-gather | bytes 557056 | tf_op jit(solution)/shard_map/all_gather | solution.py:213
  1518.1 2.1 fusion.123
  1522.7 83.8 %all-reduce.30.cloned.1.call-done = bf16[256,1024]{1,0:T(8,128)(2,1)} async-done(((bf16[256,1024]{1,0:T(8,128)(2,1)}), bf16[256,1024]{1,0:T(8,128)(2,1)}) %all-reduce.30.cloned.1.call-update) | async-done | bytes 524304 | tf_op jit(solution)/shard_map/psum | solution.py:160
  1606.5 2.0 fusion.59
  1611.2 2.7 collective-permute-start.15
  1618.7 71.1 %reduce-scatter.27.cloned.1.call-done = bf16[16,1024]{1,0:T(8,128)(2,1)} async-done(((bf16[256,1024]{1,0:T(8,128)(2,1)}), bf16[16,1024]{1,0:T(8,128)(2,1)}) %reduce-scatter.27.cloned.1.call-update) | async-done | bytes 32784 | tf_op jit(solution)/shard_map/reduce_scatter | solution.py:196
  1692.8 2.6 convolution_select_fusion.4
  1695.3 23.3 %all_gather.31 = bf16[256,1024]{1,0:T(8,128)(2,1)S(1)} all-gather(bf16[16,1024]{1,0:T(8,128)(2,1)S(1)} %collective-permute-done.16), channel_id=1, replica_groups=mesh['section'=2,'seq'=4,'wa'=16] {'wa'}, dimensions={0}, use_global_device_ids=true | all-gather | bytes 557056 | tf_op jit(solution)/shard_map/all_gather | solution.py:213
  1718.7 1.8 fusion.115
  1722.7 2.5 fusion.77
  1725.2 3.3 fusion.257
  1730.3 2.0 fusion.256
  1736.3 2.0 fusion.255
  1741.8 2.0 fusion.254
  1746.1 60.9 %all-reduce.32.cloned.1.call-done = bf16[256,1024]{1,0:T(8,128)(2,1)} async-done(((bf16[256,1024]{1,0:T(8,128)(2,1)}), bf16[256,1024]{1,0:T(8,128)(2,1)}) %all-reduce.32.cloned.1.call-update) | async-done | bytes 524304 | tf_op jit(solution)/shard_map/psum | solution.py:160
  1807.0 2.0 fusion.61
  1811.8 2.7 collective-permute-start.17
  1817.8 5.2 add_convert_fusion
  1823.1 2.6 fusion.10
  1829.5 53.5 %reduce-scatter.19.cloned.1.call-done = f32[16,1024]{1,0:T(8,128)} async-done(((f32[256,1024]{1,0:T(8,128)}), f32[16,1024]{1,0:T(8,128)}) %reduce-scatter.19.cloned.1.call-update) | async-done | bytes 65552 | tf_op jit(solution)/shard_map/reduce_scatter | solution.py:95
  1884.8 10.5 all-reduce
  1896.4 61.2 %reduce-scatter.29.cloned.1.call-done = bf16[16,1024]{1,0:T(8,128)(2,1)} async-done(((bf16[256,1024]{1,0:T(8,128)(2,1)}), bf16[16,1024]{1,0:T(8,128)(2,1)}) %reduce-scatter.29.cloned.1.call-update) | async-done | bytes 32784 | tf_op jit(solution)/shard_map/reduce_scatter | solution.py:196
  1959.2 63.4 %all-reduce.34.cloned.1.call-done = (bf16[1,1024,3,64]{1,3,2,0:T(8,128)(2,1)}, bf16[1,64,1024]{2,1,0:T(8,128)(2,1)}, bf16[1,1024,2,288]{1,3,2,0:T(8,128)(2,1)}, bf16[1,288,1024]{2,1,0:T(8,128)(2,1)}) async-done(((bf16[1,1024,3,64]{1,3,2,0:T(8,128)(2,1)}, bf16[1,64,1024]{2,1,0:T(8,128)(2,1)}, bf16[1,1024,2,288]{1,3,2,0:T(8,128)(2,1)}, bf16[1,288,1024]{2,1,0:T(8,128)(2,1)}), ...) | async-done | bytes 2293776 | tf_op jit(solution)/shard_map/psum | solution.py:219
  2024.3 2.0 reshape.348
  (562 shorter events, 157.5 us)
Async XLA Ops:
  7.2 100.3 %copy-start = (bf16[1,1024,2,288]{1,3,2,0:T(8,128)(2,1)S(1)}, bf16[1,1024,2,288]{1,3,2,0:T(8,128)(2,1)}, u32[]{:S(2)}) copy-start(bf16[1,1024,2,288]{1,3,2,0:T(8,128)(2,1)} %param.14) | copy-start | bytes 3538948
  7.2 98.1 %all-reduce.14.cloned.1.call-start = ((), (), s32[]{:S(2)}) async-start(), calls=%async_computation.10 | async-start | bytes 2097152 | tf_op jit(solution)/shard_map/psum | solution.py:80
  8.9 5.0 collective-permute-start
  16.7 90.8 %copy-start.56 = (f32[1,1024]{1,0:T(1,128)S(1)}, f32[1,1024]{1,0:T(1,128)}, u32[]{:S(2)}) copy-start(f32[1,1024]{1,0:T(1,128)} %param.13) | copy-start | bytes 12292
  16.7 165.6 %reduce-scatter.11.cloned.1.call-start = ((), (), s32[]{:S(2)}) async-start(), calls=%async_computation.11 | async-start | bytes 1114112 | tf_op jit(solution)/shard_map/reduce_scatter | solution.py:95
  106.9 75.5 %copy-start.10 = (f32[256,1024]{1,0:T(8,128)}, f32[256,1024]{1,0:T(8,128)S(1)}, u32[]{:S(2)}) copy-start(f32[256,1024]{1,0:T(8,128)S(1)} %get-tuple-element.79) | copy-start | bytes 3145732
  110.0 99.8 %copy-start.1 = (bf16[1,1024,3,64]{1,3,2,0:T(8,128)(2,1)S(1)}, bf16[1,1024,3,64]{1,3,2,0:T(8,128)(2,1)}, u32[]{:S(2)}) copy-start(bf16[1,1024,3,64]{1,3,2,0:T(8,128)(2,1)} %param.10) | copy-start | bytes 1179652
  110.1 192.6 %all-reduce.16.cloned.1.call-start = ((), (), s32[]{:S(2)}) async-start(), calls=%async_computation.12 | async-start | bytes 2097152 | tf_op jit(solution)/shard_map/psum | solution.py:80
  183.2 2.1 collective-permute-start.1
  210.2 5.0 collective-permute-start.2
  218.0 162.0 %reduce-scatter.13.cloned.1.call-start = ((), (), s32[]{:S(2)}) async-start(), calls=%async_computation.13 | async-start | bytes 1114112 | tf_op jit(solution)/shard_map/reduce_scatter | solution.py:95
  307.6 198.6 %all-reduce.18.cloned.1.call-start = ((), (), s32[]{:S(2)}) async-start(), calls=%async_computation.14 | async-start | bytes 2097152 | tf_op jit(solution)/shard_map/psum | solution.py:80
  380.8 2.1 collective-permute-start.3
  410.6 5.3 collective-permute-start.4
  421.5 162.2 %reduce-scatter.15.cloned.1.call-start = ((), (), s32[]{:S(2)}) async-start(), calls=%async_computation.15 | async-start | bytes 1114112 | tf_op jit(solution)/shard_map/reduce_scatter | solution.py:95
  511.4 198.6 %all-reduce.20.cloned.1.call-start = ((), (), s32[]{:S(2)}) async-start(), calls=%async_computation.16 | async-start | bytes 2097152 | tf_op jit(solution)/shard_map/psum | solution.py:80
  584.6 2.1 collective-permute-start.5
  614.3 5.3 collective-permute-start.6
  625.3 162.2 %reduce-scatter.17.cloned.1.call-start = ((), (), s32[]{:S(2)}) async-start(), calls=%async_computation.17 | async-start | bytes 1114112 | tf_op jit(solution)/shard_map/reduce_scatter | solution.py:95
  715.2 198.7 %all-reduce.22.cloned.1.call-start = ((), (), s32[]{:S(2)}) async-start(), calls=%async_computation.18 | async-start | bytes 2097152 | tf_op jit(solution)/shard_map/psum | solution.py:80
  788.4 2.1 collective-permute-start.7
  818.1 5.3 collective-permute-start.8
  829.1 177.2 %all-reduce.24.cloned.1.call-start = ((), (), s32[]{:S(2)}) async-start(), calls=%async_computation.20 | async-start | bytes 1048576 | tf_op jit(solution)/shard_map/psum | solution.py:160
  921.7 168.4 %reduce-scatter.21.cloned.1.call-start = ((), (), s32[]{:S(2)}) async-start(), calls=%async_computation.21 | async-start | bytes 557056 | tf_op jit(solution)/shard_map/reduce_scatter | solution.py:196
  1011.4 4.3 collective-permute-start.9
  1017.7 188.6 %all-reduce.26.cloned.1.call-start = ((), (), s32[]{:S(2)}) async-start(), calls=%async_computation.22 | async-start | bytes 1048576 | tf_op jit(solution)/shard_map/psum | solution.py:160
  1091.5 3.1 collective-permute-start.10
  1122.2 168.0 %reduce-scatter.23.cloned.1.call-start = ((), (), s32[]{:S(2)}) async-start(), calls=%async_computation.23 | async-start | bytes 557056 | tf_op jit(solution)/shard_map/reduce_scatter | solution.py:196
  1211.5 4.3 collective-permute-start.11
  1217.8 188.6 %all-reduce.28.cloned.1.call-start = ((), (), s32[]{:S(2)}) async-start(), calls=%async_computation.24 | async-start | bytes 1048576 | tf_op jit(solution)/shard_map/psum | solution.py:160
  1291.7 3.1 collective-permute-start.12
  1322.3 168.0 %reduce-scatter.25.cloned.1.call-start = ((), (), s32[]{:S(2)}) async-start(), calls=%async_computation.25 | async-start | bytes 557056 | tf_op jit(solution)/shard_map/reduce_scatter | solution.py:196
  1411.6 4.3 collective-permute-start.13
  1417.9 188.6 %all-reduce.30.cloned.1.call-start = ((), (), s32[]{:S(2)}) async-start(), calls=%async_computation.26 | async-start | bytes 1048576 | tf_op jit(solution)/shard_map/psum | solution.py:160
  1491.8 3.1 collective-permute-start.14
  1522.4 167.5 %reduce-scatter.27.cloned.1.call-start = ((), (), s32[]{:S(2)}) async-start(), calls=%async_computation.27 | async-start | bytes 557056 | tf_op jit(solution)/shard_map/reduce_scatter | solution.py:196
  1611.2 4.3 collective-permute-start.15
  1617.5 189.5 %all-reduce.32.cloned.1.call-start = ((), (), s32[]{:S(2)}) async-start(), calls=%async_computation.28 | async-start | bytes 1048576 | tf_op jit(solution)/shard_map/psum | solution.py:160
  1691.4 4.0 collective-permute-start.16
  1722.6 160.3 %reduce-scatter.19.cloned.1.call-start = ((), (), s32[]{:S(2)}) async-start(), calls=%async_computation.19 | async-start | bytes 1114112 | tf_op jit(solution)/shard_map/reduce_scatter | solution.py:95
  1728.5 229.1 %reduce-scatter.29.cloned.1.call-start = ((), (), s32[]{:S(2)}) async-start(), calls=%async_computation.29 | async-start | bytes 557056 | tf_op jit(solution)/shard_map/reduce_scatter | solution.py:196
  1745.2 61.8 %copy-start.11 = (f32[256,1024]{1,0:T(8,128)S(1)}, f32[256,1024]{1,0:T(8,128)}, u32[]{:S(2)}) copy-start(f32[256,1024]{1,0:T(8,128)} %copy-done.10) | copy-start | bytes 3145732
  1745.2 61.8 %copy-start.144 = (f32[256]{0:T(256)S(1)}, f32[256]{0:T(256)}, u32[]{:S(2)}) copy-start(f32[256]{0:T(256)} %copy-done.143) | copy-start | bytes 3076
  1746.1 63.0 %copy-start.156 = (f32[256]{0:T(256)S(1)}, f32[256]{0:T(256)}, u32[]{:S(2)}) copy-start(f32[256]{0:T(256)} %get-tuple-element.104) | copy-start | bytes 3076
  1811.8 4.3 collective-permute-start.17
  1817.5 205.1 %all-reduce.34.cloned.1.call-start = ((), (), s32[]{:S(2)}) async-start(), calls=%async_computation.30 | async-start | bytes 4587520 | tf_op jit(solution)/shard_map/psum | solution.py:219
  1829.2 55.3 %copy-start.151 = (f32[1024]{0:T(1024)S(1)}, f32[1024]{0:T(1024)}, u32[]{:S(2)}) copy-start(f32[1024]{0:T(1024)} %get-tuple-element.16) | copy-start | bytes 12292
  1829.2 55.3 %copy-start.157 = (f32[64]{0:T(128)S(1)}, f32[64]{0:T(128)}, u32[]{:S(2)}) copy-start(f32[64]{0:T(128)} %get-tuple-element.26) | copy-start | bytes 772
  1829.3 55.3 %copy-start.158 = (f32[64]{0:T(128)S(1)}, f32[64]{0:T(128)}, u32[]{:S(2)}) copy-start(f32[64]{0:T(128)} %get-tuple-element.27) | copy-start | bytes 772
  1829.3 55.3 %copy-start.159 = (f32[64]{0:T(128)S(1)}, f32[64]{0:T(128)}, u32[]{:S(2)}) copy-start(f32[64]{0:T(128)} %get-tuple-element.28) | copy-start | bytes 772
  1829.3 55.3 %copy-start.160 = (f32[64]{0:T(128)S(1)}, f32[64]{0:T(128)}, u32[]{:S(2)}) copy-start(f32[64]{0:T(128)} %get-tuple-element.29) | copy-start | bytes 772
  1829.3 55.3 %copy-start.161 = (f32[64]{0:T(128)S(1)}, f32[64]{0:T(128)}, u32[]{:S(2)}) copy-start(f32[64]{0:T(128)} %get-tuple-element.30) | copy-start | bytes 772
  1829.3 55.3 %copy-start.162 = (f32[64]{0:T(128)S(1)}, f32[64]{0:T(128)}, u32[]{:S(2)}) copy-start(f32[64]{0:T(128)} %get-tuple-element.31) | copy-start | bytes 772
  1829.3 55.3 %copy-start.163 = (f32[64]{0:T(128)S(1)}, f32[64]{0:T(128)}, u32[]{:S(2)}) copy-start(f32[64]{0:T(128)} %get-tuple-element.32) | copy-start | bytes 772
  1829.3 55.3 %copy-start.164 = (f32[64]{0:T(128)S(1)}, f32[64]{0:T(128)}, u32[]{:S(2)}) copy-start(f32[64]{0:T(128)} %get-tuple-element.33) | copy-start | bytes 772
  1829.3 55.3 %copy-start.165 = (f32[64]{0:T(128)S(1)}, f32[64]{0:T(128)}, u32[]{:S(2)}) copy-start(f32[64]{0:T(128)} %get-tuple-element.34) | copy-start | bytes 772
  1829.3 55.3 %copy-start.166 = (f32[64]{0:T(128)S(1)}, f32[64]{0:T(128)}, u32[]{:S(2)}) copy-start(f32[64]{0:T(128)} %get-tuple-element.35) | copy-start | bytes 772
  1829.3 55.3 %copy-start.167 = (f32[64]{0:T(128)S(1)}, f32[64]{0:T(128)}, u32[]{:S(2)}) copy-start(f32[64]{0:T(128)} %get-tuple-element.36) | copy-start | bytes 772
  1829.4 55.3 %copy-start.168 = (f32[64]{0:T(128)S(1)}, f32[64]{0:T(128)}, u32[]{:S(2)}) copy-start(f32[64]{0:T(128)} %get-tuple-element.37) | copy-start | bytes 772
  1829.4 55.3 %copy-start.169 = (f32[64]{0:T(128)S(1)}, f32[64]{0:T(128)}, u32[]{:S(2)}) copy-start(f32[64]{0:T(128)} %get-tuple-element.38) | copy-start | bytes 772
  1829.4 129.0 %copy-start.117 = (f32[1,16,1024]{2,1,0:T(8,128)S(1)}, f32[1,16,1024]{2,1,0:T(8,128)}, u32[]{:S(2)}) copy-start(f32[1,16,1024]{2,1,0:T(8,128)} %get-tuple-element.84) | copy-start | bytes 196612
  1829.4 129.0 %copy-start.118 = (f32[1,16,1024]{2,1,0:T(8,128)S(1)}, f32[1,16,1024]{2,1,0:T(8,128)}, u32[]{:S(2)}) copy-start(f32[1,16,1024]{2,1,0:T(8,128)} %get-tuple-element.86) | copy-start | bytes 196612
  1829.4 129.0 %copy-start.119 = (f32[1,16,1024]{2,1,0:T(8,128)S(1)}, f32[1,16,1024]{2,1,0:T(8,128)}, u32[]{:S(2)}) copy-start(f32[1,16,1024]{2,1,0:T(8,128)} %get-tuple-element.88) | copy-start | bytes 196612
  1829.4 129.0 %copy-start.120 = (f32[1,16,1024]{2,1,0:T(8,128)S(1)}, f32[1,16,1024]{2,1,0:T(8,128)}, u32[]{:S(2)}) copy-start(f32[1,16,1024]{2,1,0:T(8,128)} %get-tuple-element.83) | copy-start | bytes 196612
  (148 other events, 889.4 us)
Sparse Core Ops, SparseCore 0:
  16.8 88.3 all-reduce.13
  110.2 72.1 reduce-scatter.10
  218.1 84.5 all-reduce.15
  307.8 72.1 reduce-scatter.12
  421.7 84.5 all-reduce.17
  511.5 72.1 reduce-scatter.14
  625.4 84.5 all-reduce.19
  715.3 72.2 reduce-scatter.16
  829.2 84.5 all-reduce.21
  921.8 84.4 all-reduce.23
  1017.8 72.1 reduce-scatter.20
  1122.3 83.8 all-reduce.25
  1217.9 72.2 reduce-scatter.22
  1322.5 83.9 all-reduce.27
  1418.1 72.1 reduce-scatter.24
  1522.5 83.9 all-reduce.29
  1617.6 72.1 reduce-scatter.26
  1722.8 84.2 all-reduce.31
  1810.6 72.3 reduce-scatter.18
  1885.9 71.5 reduce-scatter.28
  1961.0 61.5 all-reduce.33
where the time goes:
time: 2040 us
  waiting for transfers between devices  1610 us (79%)
  blocking collectives  197 us (10%)
  matrix products  80.8 us (4%)
  other arithmetic  67.3 us (3%)
  starting transfers between devices  32.9 us (2%)
  local copies, waits for them, and re-layouts  28.3 us (1%)
    psum x5, waiting for transfers between devices, body(): lax.psum(jnp.dot(mixed_in, out_matrix, preferred_element_type=jnp.float32...  427 us
    psum x5, waiting for transfers between devices, body(): lax.psum(contract_last(gate_up_bf, gate_up).astype(jnp.bfloat16), 'wa')  397 us
    reduce_scatter x5, waiting for transfers between devices, body(): lax.psum_scatter(contract_last(proj_bf, in_matrix).astype(jnp.bfloat16),...  349 us
    reduce_scatter x5, waiting for transfers between devices, body(): lax.psum_scatter(jnp.dot(hidden, down_matrix, preferred_element_type=jnp....  343 us
    all_gather x4, blocking collectives, body(): received = lax.all_gather(arrived, 'wa', axis=0, tiled=True)  93.4 us
    all_gather x4, blocking collectives, body(): lax.all_gather(arrived_grad.astype(jnp.bfloat16), 'wa', axis=0, tiled=True)  93.1 us
    psum x1, waiting for transfers between devices, body(): lax.psum(in_total.astype(jnp.bfloat16), 'seq').astype(jnp.float32)  63.4 us
  transfers between devices with their start and end apart: 39, of which 38 were waited for; matrix products, arithmetic and copies ran while one was open for 2% of the time, Pallas kernels for 0%

commit v1 on v0

v1 whole, which is shorter than its diff:
```python
import functools
import types

import jax
import jax.numpy as jnp
from jax import lax
from jax.experimental import pallas as pl
from jax.experimental.pallas import tpu as pltpu
from jax.sharding import PartitionSpec as P

EPSILON = 1e-05
MESH = pl.DeviceIdType.MESH
BF = jnp.bfloat16
F32 = jnp.float32
ROWS = 16
CHUNKS = 2


def dot_nn(a, b):
    return jnp.dot(a, b, preferred_element_type=F32)


def dot_nt(a, b):
    return lax.dot_general(a, b, (((1,), (1,)), ((), ())), preferred_element_type=F32)


def dot_tn(a, b):
    return lax.dot_general(a, b, (((0,), (0,)), ((), ())), preferred_element_type=F32)


def tiles(total, size=256):
    return [(start, min(size, total - start)) for start in range(0, total, size)]


def row_loop(total, step, fn):
    def it(i, carry):
        fn(pl.ds(pl.multiple_of(i * step, step), step))
        return carry

    lax.fori_loop(0, total // step, it, 0)


def kernel(cfg, names, *refs):
    NX, NW, T, D, LW, HW, HP = cfg
    r = types.SimpleNamespace(**dict(zip(names, refs, strict=True)))
    c = lax.axis_index("section")
    x = lax.axis_index("seq")
    w = lax.axis_index("wa")
    last = (x + 1) // NX
    first = (NX - x) // NX
    own = pl.ds(pl.multiple_of(w * ROWS, ROWS), ROWS)
    core_peer = (1 - c, x, w)
    NY = NZ = next(i for i in range(1, NW + 1) if i * i >= NW)
    z = w // NY
    y = w - z * NY
    LO, HI = pl.ds(0, D // 2), pl.ds(D // 2, D // 2)
    w_last = (w + 1) // NW
    w_first = (NW - w) // NW
    end = last * w_last
    begin = first * w_first
    next_dev = (c + end * (1 - 2 * c), lax.rem(x + w_last, NX), lax.rem(w + 1, NW))
    prev_dev = (c + begin * (1 - 2 * c), lax.rem(x + NX - w_first, NX), lax.rem(w + NW - 1, NW))

    def y_at(i):
        return lax.rem(y + i, NY)

    def z_at(i):
        return lax.rem(z + i, NZ)

    def y_peer(i):
        return (c, x, z * NY + y_at(i))

    def z_peer(i):
        return (c, x, z_at(i) * NY + y)

    def flat(ref, *cols):
        value = ref[(slice(None),) * 3 + cols] if cols else ref[...]
        return value.reshape(T, value.shape[-1])

    def wa_peer(i):
        return (c, x, lax.rem(w + i, NW))

    def x_peer(i):
        return (c, lax.rem(x + i, NX), w)

    def remote(src, dst, send, recv, dev):
        return pltpu.make_async_remote_copy(
            src_ref=src, dst_ref=dst, send_sem=send, recv_sem=recv, device_id=dev, device_id_type=MESH
        )

    def await_bytes(ref, sem):
        pltpu.make_async_copy(ref, ref, sem).wait()

    loads = []

    def load(src, dst):
        cp = pltpu.make_async_copy(src, dst, r.lsem.at[len(loads)])
        cp.start()
        loads.append(cp)
        return len(loads) - 1

    wpairs = [
        (r.w_in, r.Cown.at[c, pl.ds(0, 3)]),
        (r.w_small, r.Wsm.at[c]),
        (r.w_gu, r.Wgu.at[c, :, pl.ds(0, HW)]),
        (r.w_dn, r.Wdn.at[c, pl.ds(0, HW)]),
        (r.w_out, r.Cown.at[c, 3]),
    ]
    l_tok = [load(r.tokens.at[c], r.tok.at[0]), None]
    l_w = [load(*wpairs[0]), load(*wpairs[1])]
    l_tok[1] = load(r.tokens.at[2 + c], r.tok.at[1])
    l_w += [load(*p) for p in wpairs[2:]]
    l_cot = [load(r.cotangent.at[2 * k + c], r.cot.at[k]) for k in range(CHUNKS)]

    bar = pltpu.get_barrier_semaphore()

    def sig(dev):
        pl.semaphore_signal(bar, inc=1, device_id=dev, device_id_type=MESH)

    sig(core_peer)

    def sig_wa(i, carry):
        sig(wa_peer(i))
        return carry

    lax.fori_loop(1, NW, sig_wa, 0)
    for i in range(1, NX):
        sig(x_peer(i))
    sig((1 - c, lax.rem(x + 1, NX), w))
    sig((1 - c, lax.rem(x + NX - 1, NX), w))
    sig(next_dev)
    sig(prev_dev)
    if HP > HW:
        for l in range(2):
            r.Wdn[l, HW:] = jnp.zeros((HP - HW, D), BF)
            r.Wgu[l, :, HW:] = jnp.zeros((2, HP - HW, D), BF)
    r.gacc[...] = jnp.zeros(r.gacc.shape, F32)
    r.tacc[...] = jnp.zeros(r.tacc.shape, F32)
    pl.semaphore_wait(bar, (NW - 1) + (NX - 1) + 5)

    wcopies = []
    for i, (src, dst) in enumerate(wpairs):
        cp = remote(src, dst, r.wsend.at[i], r.wrecv.at[i], core_peer)
        cp.start()
        wcopies.append(cp)
    wready = set()

    def need_w(i):
        if i not in wready:
            wready.add(i)
            loads[l_w[i]].wait()
            wcopies[i].wait_recv()

    full = r.Cfull
    HALF = D // 2
    LQ = LW // NX
    xrows = pl.ds(pl.multiple_of(x * LQ, LQ), LQ)
    clanes = pl.ds(pl.multiple_of(c * HALF, HALF), HALF)
    la, lb = (pl.ds(pl.multiple_of(c * HALF + h, HALF // 2), HALF // 2) for h in (0, HALF // 2))
    first_a, first_b = full.at[:, 0, 0 : NY - 1, xrows, la], full.at[:, 0 : NZ - 1, 0, xrows, lb]
    second_a, second_b = full.at[:, 0 : NZ - 1, :, xrows, la], full.at[:, :, 0 : NY - 1, xrows, lb]

    def gather_wa():
        need_w(0)
        need_w(1)
        need_w(4)
        local = pltpu.make_async_copy(
            r.Cown.at[1, :, xrows, clanes], full.at[:, z, y, xrows, clanes], r.gwsem.at[0]
        )
        local.start()
        for lanes, peer, count, sem in ((la, y_peer, NY, 1), (lb, z_peer, NZ, 5)):
            for i in range(1, count):
                remote(
                    r.Cown.at[1, :, xrows, lanes], full.at[:, z, y, xrows, lanes],
                    r.gwsem.at[sem], r.gwsem.at[sem + 1], peer(i),
                ).start()
        tap = r.Wsm.at[1, :, pl.ds(0, 128)]
        tap_dst = r.taps1.at[w]
        tap_dst[...] = tap[...]

        def it(i, carry):
            remote(tap, tap_dst, r.gwsem.at[3], r.gwsem.at[4], wa_peer(i)).start()
            return carry

        lax.fori_loop(1, NW, it, 0)
        local.wait()

    def gather_mid():
        await_bytes(first_a, r.gwsem.at[2])
        piece = full.at[:, z, :, xrows, la]
        for i in range(1, NZ):
            remote(piece, piece, r.gwsem.at[7], r.gwsem.at[8], z_peer(i)).start()
        await_bytes(first_b, r.gwsem.at[6])
        piece = full.at[:, :, y, xrows, lb]
        for i in range(1, NY):
            remote(piece, piece, r.gwsem.at[9], r.gwsem.at[10], y_peer(i)).start()

    def gather_x(p):
        if p == 0:
            await_bytes(second_a, r.gwsem.at[8])
            await_bytes(second_b, r.gwsem.at[10])
        piece = full.at[p, :, :, xrows, clanes]
        for j in range(1, NX):
            remote(piece, piece, r.gxs.at[p], r.gxr.at[p], x_peer(j)).start()

    def gather_core(p):
        await_bytes(full.at[p, :, :, pl.ds(0, (NX - 1) * LQ), clanes], r.gxr.at[p])
        piece = full.at[p, :, :, :, clanes]
        remote(piece, piece, r.gcs.at[p], r.gcr.at[p], core_peer).start()

    def gather_done(p):
        await_bytes(full.at[p, :, :, :, clanes], r.gcr.at[p])

    def gather_close():
        for ref, sem in ((first_a, 1), (first_b, 5), (second_a, 7), (second_b, 9)):
            await_bytes(ref, r.gwsem.at[sem])
        await_bytes(r.taps1.at[pl.ds(0, NW - 1)], r.gwsem.at[3])
        for p in range(4):
            await_bytes(full.at[p, :, :, pl.ds(0, (NX - 1) * LQ), clanes], r.gxs.at[p])
            await_bytes(full.at[p, :, :, :, clanes], r.gcs.at[p])

    counts = {"ag": 0, "rs": 0}
    ag_sent, rs_sent = [], []

    def ag_start(buf):
        n = counts["ag"]
        counts["ag"] += 1
        lo, hi = buf.at[z, y, :, LO], buf.at[z, y, :, HI]
        for i in range(1, NY):
            remote(lo, lo, r.ags.at[n, 0], r.agr.at[n, 0], y_peer(i)).start()
            remote(hi, hi, r.ags.at[n, 1], r.agr.at[n, 1], z_peer(i)).start()
        ag_sent.append((n, buf))
        return n

    def ag_first(buf):
        return buf.at[0, pl.ds(0, NY - 1), :, LO]

    def ag_second(buf):
        return buf.at[pl.ds(0, NZ - 1), :, :, LO]

    def ag_mid(n, buf):
        lo, hi = buf.at[z, :, :, LO], buf.at[:, y, :, HI]
        await_bytes(ag_first(buf), r.agr.at[n, 0])
        for i in range(1, NZ):
            remote(lo, lo, r.ags.at[n, 2], r.agr.at[n, 2], z_peer(i)).start()
        await_bytes(ag_first(buf), r.agr.at[n, 1])
        for i in range(1, NY):
            remote(hi, hi, r.ags.at[n, 3], r.agr.at[n, 3], y_peer(i)).start()

    def ag_wait(n, buf):
        for i in (2, 3):
            await_bytes(ag_second(buf), r.agr.at[n, i])

    stage_use = [[], []]

    def stage_get(k):
        uses = stage_use[k]
        slot = len(uses) % 2
        if len(uses) >= 2:
            stage_sent(*uses[-2])
        return r.stage.at[k, slot]

    def stage_sent(n, buf):
        for i in (0, 1):
            await_bytes(ag_second(buf), r.rss.at[n, i])

    def rs_start(k, buf):
        n = counts["rs"]
        counts["rs"] += 1
        for i in range(1, NY):
            remote(
                buf.at[:, y_at(i), :, LO], r.rva.at[n, y], r.rss.at[n, 0], r.rsr.at[n, 0], y_peer(i)
            ).start()
            remote(
                buf.at[z_at(i), :, :, HI], r.rvb.at[n, z], r.rss.at[n, 1], r.rsr.at[n, 1], z_peer(i)
            ).start()
        stage_use[k].append((n, buf))
        return n

    def rs_mid(n, k):
        buf = dict(stage_use[k])[n]
        sa, sb = r.rsa.at[n], r.rsb.at[n]
        await_bytes(r.rva.at[n, pl.ds(0, NY - 1)], r.rsr.at[n, 0])
        total = buf[:, y, :, LO].astype(F32)
        for i in range(1, NY):
            total = total + r.rva[n, y_at(i)].astype(F32)
        sa[...] = total.astype(BF)
        for i in range(1, NZ):
            remote(sa.at[z_at(i)], r.rwa.at[n, z], r.rss.at[n, 2], r.rsr.at[n, 2], z_peer(i)).start()
        await_bytes(r.rvb.at[n, pl.ds(0, NZ - 1)], r.rsr.at[n, 1])
        total = buf[z, :, :, HI].astype(F32)
        for i in range(1, NZ):
            total = total + r.rvb[n, z_at(i)].astype(F32)
        sb[...] = total.astype(BF)
        for i in range(1, NY):
            remote(sb.at[y_at(i)], r.rwb.at[n, y], r.rss.at[n, 3], r.rsr.at[n, 3], y_peer(i)).start()

    def rs_sum(n):
        await_bytes(r.rwa.at[n, pl.ds(0, NZ - 1)], r.rsr.at[n, 2])
        lo = r.rsa[n, z].astype(F32)
        for i in range(1, NZ):
            lo = lo + r.rwa[n, z_at(i)].astype(F32)
        await_bytes(r.rwb.at[n, pl.ds(0, NY - 1)], r.rsr.at[n, 3])
        hi = r.rsb[n, y].astype(F32)
        for i in range(1, NY):
            hi = hi + r.rwb[n, y_at(i)].astype(F32)
        return jnp.concatenate([lo, hi], 1)

    def mids(kind, l, name, ks):
        for k in ks:
            if kind == "rs":
                rs_mid(rs_id[name, l, k], k)
            else:
                key, buf = {
                    "n": (("n", l, k), r.norm.at[l, k]),
                    "u": (("u", k), r.u1.at[k]),
                    "r": (("r", l, k), r.rb.at[l, k]),
                    "g": (("g", k), r.gbf.at[k]),
                }[name]
                ag_mid(ag_id[key], buf)

    rs_id, ag_id = {}, {}

    def u_of(l, k):
        return r.tok.at[k] if l == 0 else r.u1.at[k]

    hcopy = {}

    w0 = r.Cown.at[0]

    def put(ref, n0, n, value):
        ref[:, :, :, n0 : n0 + n] = value.astype(BF).reshape(NZ, NY, ROWS, n)

    def s1(l, k):
        u = u_of(l, k)
        loads[l_tok[k]].wait()
        need_w(0)
        projected = dot_nt(u[...], w0[0:3].reshape(3 * LW, D))
        b_part = projected[:, :LW]
        x_part = projected[:, 2 * LW :]
        r.projB[k] = b_part
        r.projC[k] = projected[:, LW : 2 * LW]
        r.projX[k] = x_part
        gated = (b_part * x_part).astype(BF)
        r.gp[k, pl.ds(8, T)] = gated.astype(F32)
        r.hs[k] = gated[T - 16 :]

        slot = k + last * c

        def send():
            remote(
                r.hs.at[k],
                r.hb.at[slot],
                r.hsend.at[k],
                r.hrecv.at[slot],
                (c + last * (1 - 2 * c), lax.rem(x + 1, NX), w),
            ).start()

        if k == CHUNKS - 1:
            pl.when(last * c == 0)(send)
        else:
            send()

    def s2(l, k):
        def get():
            await_bytes(r.hb.at[k], r.hrecv.at[k])

        def zero():
            r.hb[k] = jnp.zeros((16, LW), BF)

        if k == 0:
            none = first * (1 - c)
            pl.when(none == 0)(get)
            pl.when(none == 1)(zero)
        else:
            get()
        need_w(1)
        need_w(4)
        r.gp[k, pl.ds(0, 8)] = r.hb[k].astype(F32)[8:]
        taps = r.Wsm[l]
        conv = (
            taps[1:2, :LW] * r.gp[k, pl.ds(6, T)]
            + taps[2:3, :LW] * r.gp[k, pl.ds(7, T)]
            + taps[3:4, :LW] * r.gp[k, pl.ds(8, T)]
        )
        r.conv[k] = conv
        r.mixed[k] = (r.projC[k] * conv).astype(BF)
        buf = stage_get(k)
        for n0, n in tiles(D):
            put(buf, n0, n, dot_nn(r.mixed[k], w0[3, :, n0 : n0 + n]))
        rs_id["a", l, k] = rs_start(k, buf)

    def inv_rms(res):
        return lax.rsqrt(jnp.mean(res * res, -1, keepdims=True) + EPSILON)

    def s3(l, k):
        res = r.tok[k, own].astype(F32) + rs_sum(rs_id["a", l, k])
        r.res[l, k] = res
        buf = r.norm.at[l, k]
        buf[z, y] = (res * inv_rms(res) * r.Wsm[l, 0:1]).astype(BF)
        ag_id["n", l, k] = ag_start(buf)

    def s4(l, k):
        buf = r.norm.at[l, k]
        ag_wait(ag_id["n", l, k], buf)
        need_w(2)
        need_w(3)
        gu = r.gu.at[l, k]
        for g in range(2):
            gu[:, g * HP : (g + 1) * HP] = dot_nt(flat(buf), r.Wgu[l, g])

        def act(rows):
            gate = gu[rows, :HP]
            up = gu[rows, HP:]
            r.hid[l, k, rows] = (gate * jax.nn.sigmoid(gate) * up).astype(BF)

        row_loop(T, 32, act)
        st = stage_get(k)
        for n0, n in tiles(D):
            put(st, n0, n, dot_nn(r.hid[l, k], r.Wdn[l, :, n0 : n0 + n]))
        rs_id["b", l, k] = rs_start(k, st)

    def emit(l, k, value, staging, target, sems):
        staging[l, k] = value

        @pl.when(c == l)
        def _():
            target[2 * k + c] = value

        @pl.when(c != l)
        def _():
            remote(
                staging.at[l, k],
                target.at[2 * k + c],
                r.osend.at[sems, k],
                r.orecv.at[sems, k],
                core_peer,
            ).start()

    def s5(l, k):
        rows = (r.res[l, k] + rs_sum(rs_id["b", l, k])).astype(BF)
        if l == 0:
            r.u1[k, z, y] = rows
        emit(l, k, rows, r.lost, r.lo, 0)

    def outbf(l, k):
        return r.cotb.at[k] if l == 1 else r.gbf.at[k]

    def prep_cot(k):
        loads[l_cot[k]].wait()

        def cast(rows):
            r.cotb[k, rows] = r.cot[k, rows].astype(BF)

        row_loop(T, 32, cast)

    def t1(l, k):
        ob = outbf(l, k)
        if l == 0:
            ag_wait(ag_id["g", k], ob)
        hg = r.hg.at[k]
        for n0, n in tiles(HP):
            hg[:, n0 : n0 + n] = dot_nt(ob[...] if l == 1 else flat(ob), r.Wdn[l, n0 : n0 + n])
        gu = r.gu.at[l, k]
        gub = r.gub.at[l, k]

        def act(rows):
            gate = gu[rows, :HP]
            up = gu[rows, HP:]
            h = hg[rows]
            s = jax.nn.sigmoid(gate)
            gub[rows, :HP] = (h * up * (s * (1.0 + gate * (1.0 - s)))).astype(BF)
            gub[rows, HP:] = (h * (gate * s)).astype(BF)

        row_loop(T, 32, act)
        st = stage_get(k)
        for n0, n in tiles(D):
            put(st, n0, n, dot_nn(gub[...], r.Wgu[l, :, :, n0 : n0 + n].reshape(2 * HP, n)))
        rs_id["c", l, k] = rs_start(k, st)

    def t2(l, k):
        ng = rs_sum(rs_id["c", l, k])
        res = r.res[l, k]
        inv = inv_rms(res)
        g = r.cot[k, own] if l == 1 else r.g0own[k]
        r.gacc[l] = r.gacc[l] + jnp.sum(ng * res * inv, 0, keepdims=True)
        scaled = ng * r.Wsm[l, 0:1]
        rg = g + inv * scaled - res * (inv * inv * inv) * jnp.mean(scaled * res, -1, keepdims=True)
        r.rg[l, k] = rg
        buf = r.rb.at[l, k]
        buf[z, y] = rg.astype(BF)
        if l == 0:
            ag_id["r", l, k] = ag_start(buf)

    def t3(l, k):
        buf = r.rb.at[l, k]
        ag_wait(ag_id["r", l, k], buf)
        mg = dot_nt(flat(buf), w0[3])
        r.pbf[k, :, LW : 2 * LW] = (mg * r.conv[k]).astype(BF)
        cvg = mg * r.projC[k]
        r.cvg[k, pl.ds(0, T)] = cvg
        r.hgs[k] = cvg[:8]
        slot = k - first * (1 - c)

        def send():
            remote(
                r.hgs.at[k],
                r.hgb.at[slot],
                r.hgsend.at[k],
                r.hgrecv.at[slot],
                (c + first * (1 - 2 * c), lax.rem(x + NX - 1, NX), w),
            ).start()

        if k == 0:
            pl.when(first * (1 - c) == 0)(send)
        else:
            send()

    def t4(l, k):
        def get():
            await_bytes(r.hgb.at[k], r.hgrecv.at[k])

        def zero():
            r.hgb[k] = jnp.zeros((8, LW), F32)

        if k == CHUNKS - 1:
            none = last * c
            pl.when(none == 0)(get)
            pl.when(none == 1)(zero)
        else:
            get()
        e = r.cvg.at[k]
        e[pl.ds(T, 8)] = r.hgb[k]
        taps = r.Wsm[l]
        gg = (
            taps[3:4, :LW] * e[pl.ds(0, T)]
            + taps[2:3, :LW] * e[pl.ds(1, T)]
            + taps[1:2, :LW] * e[pl.ds(2, T)]
        )
        pbf = r.pbf.at[k]
        pbf[:, :LW] = (gg * r.projX[k]).astype(BF)
        pbf[:, 2 * LW :] = (gg * r.projB[k]).astype(BF)
        st = stage_get(k)
        for n0, n in tiles(D):
            put(st, n0, n, dot_nn(pbf[...], w0[0:3, :, n0 : n0 + n].reshape(3 * LW, n)))
        rs_id["d", l, k] = rs_start(k, st)
        cvg = e[pl.ds(0, T)]
        for j in range(3):
            r.tacc[j : j + 1, :LW] = r.tacc[j : j + 1, :LW] + jnp.sum(
                cvg * r.gp[k, pl.ds(6 + j, T)], 0, keepdims=True
            )

    def t5(l, k):
        rows = r.rg[l, k] + rs_sum(rs_id["d", l, k])
        emit(l, k, rows, r.ligst, r.ig, 1)

    def full_in():
        return full[0:3].reshape(3 * D, D)

    def taps_row(j):
        return jnp.concatenate([r.taps1[i, j : j + 1, :LW] for i in range(NW)], 1)

    def f1a():
        u = jnp.concatenate([r.u1[k, z, y] for k in range(CHUNKS)], 0)
        for p in range(3):
            gather_done(p)
            if p == 1:
                gather_core(2)
            r.proj1[p] = dot_nt(u, full[p].reshape(D, D))
        gated = (r.proj1[0] * r.proj1[2]).astype(BF)
        for k in range(CHUNKS):
            g = gated[k * ROWS : (k + 1) * ROWS]
            r.gp1[k, pl.ds(8, ROWS)] = g.astype(F32)
            r.h1s[k] = g
            slot = k + end * c

            def send(k=k, slot=slot):
                remote(
                    r.h1s.at[k], r.h1b.at[slot], r.h1send.at[k], r.h1recv.at[slot], next_dev
                ).start()

            if k == CHUNKS - 1:
                pl.when(end * c == 0)(send)
            else:
                send()

    def f1b():
        await_bytes(r.taps1.at[pl.ds(0, NW - 1)], r.gwsem.at[4])
        r.trow[...] = jnp.concatenate([taps_row(j + 1) for j in range(3)], 0)
        for k in range(CHUNKS):

            def get(k=k):
                await_bytes(r.h1b.at[k], r.h1recv.at[k])

            def zero(k=k):
                r.h1b[k] = jnp.zeros((ROWS, D), BF)

            if k == 0:
                none = begin * (1 - c)
                pl.when(none == 0)(get)
                pl.when(none == 1)(zero)
            else:
                get()
            r.gp1[k, pl.ds(0, 8)] = r.h1b[k].astype(F32)[8:]
            conv = sum(r.trow[j : j + 1] * r.gp1[k, pl.ds(6 + j, ROWS)] for j in range(3))
            r.conv1[k] = conv
            rows = slice(k * ROWS, (k + 1) * ROWS)
            r.mixed1[rows] = (r.proj1[1, rows] * conv).astype(BF)
        gather_done(3)
        wide = dot_nn(r.mixed1[...], full[3].reshape(D, D))
        for k in range(CHUNKS):
            res = r.u1[k, z, y].astype(F32) + wide[k * ROWS : (k + 1) * ROWS]
            r.res[1, k] = res
            buf = r.norm.at[1, k]
            buf[z, y] = (res * inv_rms(res) * r.Wsm[1, 0:1]).astype(BF)
            ag_id["n", 1, k] = ag_start(buf)

    def u_start():
        for k in range(CHUNKS):
            ag_id["u", k] = ag_start(r.u1.at[k])

    def b1a():
        rb = jnp.concatenate([r.rb[1, k, z, y] for k in range(CHUNKS)], 0)
        mg = dot_nt(rb, full[3].reshape(D, D))
        for k in range(CHUNKS):
            rows = slice(k * ROWS, (k + 1) * ROWS)
            m = mg[rows]
            cvg = m * r.proj1[1, rows]
            r.cv1[k, pl.ds(0, ROWS)] = cvg
            r.pbf1[rows, D : 2 * D] = (m * r.conv1[k]).astype(BF)
            slot = k - begin * (1 - c)

            def send(k=k, slot=slot):
                remote(
                    r.cv1.at[k, pl.ds(0, 8)], r.hg1b.at[slot], r.hg1send.at[k], r.hg1recv.at[slot], prev_dev
                ).start()

            if k == 0:
                pl.when(begin * (1 - c) == 0)(send)
            else:
                send()

    def b1b():
        taps = [0.0, 0.0, 0.0]
        for k in range(CHUNKS):

            def get(k=k):
                await_bytes(r.hg1b.at[k], r.hg1recv.at[k])

            def zero(k=k):
                r.hg1b[k] = jnp.zeros((8, D), F32)

            if k == CHUNKS - 1:
                none = end * c
                pl.when(none == 0)(get)
                pl.when(none == 1)(zero)
            else:
                get()
            e = r.cv1.at[k]
            e[pl.ds(ROWS, 8)] = r.hg1b[k]
            gg = sum(r.trow[2 - j : 3 - j] * e[pl.ds(j, ROWS)] for j in range(3))
            rows = slice(k * ROWS, (k + 1) * ROWS)
            r.pbf1[rows, :D] = (gg * r.proj1[2, rows]).astype(BF)
            r.pbf1[rows, 2 * D :] = (gg * r.proj1[0, rows]).astype(BF)
            cvg = e[pl.ds(0, ROWS)]
            for j in range(3):
                taps[j] = taps[j] + jnp.sum(cvg * r.gp1[k, pl.ds(6 + j, ROWS)], 0, keepdims=True)
        r.tap1g[...] = jnp.concatenate(taps, 0)
        wide = dot_nn(r.pbf1[...], full_in())
        for k in (1, 0):
            rows = r.rg[1, k] + wide[k * ROWS : (k + 1) * ROWS]
            r.g0own[k] = rows
            u = r.gbf.at[k]
            u[z, y] = rows.astype(BF)
            ag_id["g", k] = ag_start(u)
            emit(1, k, rows, r.ligst, r.ig, 1)

    def b1_exchange():
        for k in range(CHUNKS):
            ag_id["r", 1, k] = ag_start(r.rb.at[1, k])
        for i in range(NW):
            lanes = slice(i * LW, (i + 1) * LW)
            for p in range(3):
                r.pms[i, :, p * LW : (p + 1) * LW] = r.pbf1[:, p * D + i * LW : p * D + (i + 1) * LW]
            r.pms[i, :, 3 * LW :] = r.mixed1[:, lanes]
        mine = r.pm.at[w]
        mine[...] = r.pms[w]

        def it(i, carry):
            dev = wa_peer(i)
            remote(r.pms.at[dev[2]], mine, r.pmsem.at[0], r.pmsem.at[1], dev).start()
            return carry

        lax.fori_loop(1, NW, it, 0)

    X = [r.Xgu, r.Xdn, r.Xcv]
    Y = [r.Ygu, r.Ydn, r.Ycv]
    R = [r.Rgu, r.Rdn, r.Rcv]
    O = [r.o_gu, r.o_dn, r.o_cv]
    by_row = [True, False, True]

    def part(ref, i, q):
        if by_row[i]:
            size = ref.shape[0] // NX
            return ref.at[pl.ds(pl.multiple_of(q * size, size), size)]
        size = ref.shape[1] // NX
        return ref.at[:, pl.ds(pl.multiple_of(q * size, size), size)]

    def w1(l):
        for n0, n in tiles(D):
            cols = slice(n0, n0 + n)
            for g in range(2):
                r.Xgu[l, g * HW : (g + 1) * HW, cols] = sum(
                    dot_tn(r.gub[l, k, :, g * HP : (g + 1) * HP], flat(r.norm.at[l, k], cols))
                    for k in range(CHUNKS)
                )[:HW].astype(BF)
        for n0, n in tiles(D):
            r.Xdn[l, :, n0 : n0 + n] = sum(
                dot_tn(
                    r.hid[l, k],
                    outbf(l, k)[:, n0 : n0 + n] if l == 1 else flat(outbf(l, k), slice(n0, n0 + n)),
                )
                for k in range(CHUNKS)
            )[:HW].astype(BF)

    def w2_0():
        for n0, n in tiles(D):
            cols = slice(n0, n0 + n)
            r.Xcv[0, : 3 * LW, cols] = sum(
                dot_tn(r.pbf[k], r.tok[k, :, cols]) for k in range(CHUNKS)
            ).astype(BF)
            r.Xcv[0, 3 * LW :, cols] = sum(
                dot_tn(r.mixed[k], flat(r.rb.at[0, k], cols)) for k in range(CHUNKS)
            ).astype(BF)

    def w2_1():
        await_bytes(r.pm.at[pl.ds(0, NW - 1)], r.pmsem.at[1])
        for k in range(CHUNKS):
            ag_wait(ag_id["u", k], r.u1.at[k])
            ag_wait(ag_id["r", 1, k], r.rb.at[1, k])
        pm = [r.pm[:, k * ROWS : (k + 1) * ROWS].reshape(T, 4 * LW) for k in range(CHUNKS)]
        for n0, n in tiles(D):
            cols = slice(n0, n0 + n)
            r.Xcv[1, : 3 * LW, cols] = sum(
                dot_tn(pm[k][:, : 3 * LW], flat(r.u1.at[k], cols)) for k in range(CHUNKS)
            ).astype(BF)
            r.Xcv[1, 3 * LW :, cols] = sum(
                dot_tn(pm[k][:, 3 * LW :], flat(r.rb.at[1, k], cols)) for k in range(CHUNKS)
            ).astype(BF)

    def core_send(l, i):
        @pl.when(c != l)
        def _():
            remote(X[i].at[l], Y[i], r.csend.at[i], r.crecv.at[i], core_peer).start()

    def x_reduce(l, i):
        @pl.when(c == l)
        def _():
            await_bytes(Y[i], r.crecv.at[i])
            rows_total = Y[i].shape[0]

            def add(rows):
                X[i][l, rows] = (X[i][l, rows].astype(F32) + Y[i][rows].astype(F32)).astype(BF)

            row_loop(rows_total, 32, add)
            mine = R[i].at[x]
            for j in range(1, NX):
                dev = x_peer(j)
                remote(
                    part(X[i].at[l], i, dev[1]), mine, r.xsend.at[i], r.xrecv.at[i], dev
                ).start()

    def x_gather(l, i):
        @pl.when(c == l)
        def _():
            await_bytes(R[i].at[pl.ds(0, NX - 1)], r.xrecv.at[i])
            src = part(X[i].at[l], i, x)
            R[i][x] = src[...]
            dst = part(Y[i], i, x)
            rows_total = dst.shape[0]

            def add(rows):
                total = R[i][0, rows].astype(F32)
                for j in range(1, NX):
                    total = total + R[i][j, rows].astype(F32)
                dst[rows] = total.astype(BF)

            row_loop(rows_total, 16, add)
            for j in range(1, NX):
                remote(dst, dst, r.vsend.at[i], r.vrecv.at[i], x_peer(j)).start()

    def x_finish(l, i):
        @pl.when(c == l)
        def _():
            await_bytes(R[i].at[pl.ds(0, NX - 1)], r.vrecv.at[i])
            await_bytes(R[i].at[pl.ds(0, NX - 1)], r.xsend.at[i])
            await_bytes(R[i].at[pl.ds(0, NX - 1)], r.vsend.at[i])
            pltpu.make_async_copy(Y[i], O[i], r.lsem.at[len(loads) + i]).start()

        @pl.when(c != l)
        def _():
            await_bytes(Y[i], r.csend.at[i])

    GR = D // 128

    def gain_send(l):
        st = r.gst.at[l]
        for i in range(GR):
            st[0, i : i + 1] = r.gacc[l, :, i * 128 : (i + 1) * 128]
        gain = st[0, 0:GR]
        for i in range(NW):
            st[i, 0:GR] = gain
            st[i, GR:] = jnp.zeros((8, 128), F32)
            if l == 1:
                st[i, GR : GR + 3, :LW] = r.tap1g[:, i * LW : (i + 1) * LW]
        mine = r.gex.at[l, w]
        mine[...] = st[w]

        def it(i, carry):
            dev = wa_peer(i)
            remote(st.at[dev[2]], mine, r.gsend.at[l], r.grecv.at[l], dev).start()
            return carry

        lax.fori_loop(1, NW, it, 0)

    def gain_recv(l):
        await_bytes(r.gex.at[l, pl.ds(0, NW - 1)], r.grecv.at[l])
        total = r.gex[l, 0]
        for i in range(1, NW):
            total = total + r.gex[l, i]
        r.sm[l] = total

    def small_send(l):
        if l == 0:
            r.sm[0, GR:] = r.sm[0, GR:] + r.tacc[...]

        @pl.when(c != l)
        def _():
            remote(r.sm.at[l], r.smY, r.csend.at[3], r.crecv.at[3], core_peer).start()

    def small_x(l):
        @pl.when(c == l)
        def _():
            await_bytes(r.smY, r.crecv.at[3])
            mine = r.smR.at[x]
            mine[...] = r.sm[l] + r.smY[...]
            for j in range(1, NX):
                remote(mine, mine, r.xsend.at[3], r.xrecv.at[3], x_peer(j)).start()

    def small_finish(l):
        @pl.when(c == l)
        def _():
            await_bytes(r.smR.at[pl.ds(0, NX - 1)], r.xrecv.at[3])
            total = r.smR[0]
            for j in range(1, NX):
                total = total + r.smR[j]
            r.o_small[...] = total
            await_bytes(r.smR.at[pl.ds(0, NX - 1)], r.xsend.at[3])

        @pl.when(c != l)
        def _():
            await_bytes(r.smY, r.csend.at[3])

    A, B = 0, 1
    AB, BA = (0, 1), (1, 0)
    s1(0, A)
    s1(0, B)
    gather_wa()
    s2(0, A)
    s2(0, B)
    gather_mid()
    mids("rs", 0, "a", AB)
    gather_x(0)
    s3(0, A)
    s3(0, B)
    gather_x(1)
    mids("ag", 0, "n", AB)
    s4(0, A)
    s4(0, B)
    gather_x(2)
    prep_cot(A)
    mids("rs", 0, "b", AB)
    gather_core(0)
    gather_x(3)
    prep_cot(B)
    s5(0, A)
    s5(0, B)
    gather_core(1)
    f1a()
    gather_core(3)
    f1b()
    mids("ag", 1, "n", AB)
    u_start()
    s4(1, A)
    s4(1, B)
    t1(1, B)
    mids("rs", 1, "b", AB)
    t1(1, A)
    mids("ag", 1, "u", AB)
    mids("rs", 1, "c", BA)
    w1(1)
    t2(1, B)
    t2(1, A)
    b1a()
    core_send(1, 0)
    core_send(1, 1)
    b1b()
    s5(1, A)
    s5(1, B)
    mids("ag", 0, "g", BA)
    gain_send(1)
    b1_exchange()
    x_reduce(1, 0)
    x_reduce(1, 1)
    t1(0, B)
    t1(0, A)
    w1(0)
    core_send(0, 0)
    core_send(0, 1)
    mids("rs", 0, "c", BA)
    mids("ag", 1, "r", BA)
    gain_recv(1)
    small_send(1)
    t2(0, B)
    t2(0, A)
    x_reduce(0, 0)
    x_reduce(0, 1)
    mids("ag", 0, "r", BA)
    gain_send(0)
    w2_1()
    core_send(1, 2)
    t3(0, B)
    t3(0, A)
    x_gather(1, 0)
    x_gather(1, 1)
    t4(0, B)
    t4(0, A)
    w2_0()
    core_send(0, 2)
    mids("rs", 0, "d", BA)
    x_gather(0, 0)
    x_gather(0, 1)
    x_reduce(1, 2)
    small_x(1)
    gain_recv(0)
    small_send(0)
    x_reduce(0, 2)
    small_x(0)
    t5(0, B)
    t5(0, A)
    x_gather(1, 2)
    x_gather(0, 2)
    for l in (1, 0):
        for i in range(3):
            x_finish(l, i)
        small_finish(l)
    gather_close()
    await_bytes(r.pm.at[pl.ds(0, NW - 1)], r.pmsem.at[0])

    for sems, staging, target, out in ((0, r.lost, r.lo, r.o_layer), (1, r.ligst, r.ig, r.o_grad)):
        for k in range(CHUNKS):
            await_bytes(staging.at[0, k], r.orecv.at[sems, k])
            await_bytes(staging.at[0, k], r.osend.at[sems, k])
        out[...] = target[...]
    for n, buf in ag_sent:
        for i in range(2):
            await_bytes(ag_first(buf), r.ags.at[n, i])
            await_bytes(ag_second(buf), r.ags.at[n, 2 + i])
    for uses in stage_use:
        for n, buf in uses[-2:]:
            stage_sent(n, buf)
        for n, buf in uses:
            await_bytes(r.rwa.at[n, pl.ds(0, NZ - 1)], r.rss.at[n, 2])
            await_bytes(r.rwb.at[n, pl.ds(0, NY - 1)], r.rss.at[n, 3])
    for l in range(2):
        await_bytes(r.gex.at[l, pl.ds(0, NW - 1)], r.gsend.at[l])
    for fsem, fbuf, bsem, bbuf, no_next, no_prev in (
        (r.hsend, r.hs, r.hgsend, r.hgs, last * c, first * (1 - c)),
        (r.h1send, r.h1s, r.hg1send, r.hg1b, end * c, begin * (1 - c)),
    ):
        for k in range(CHUNKS):

            def fwd(k=k, fsem=fsem, fbuf=fbuf):
                await_bytes(fbuf.at[k], fsem.at[k])

            def bwd(k=k, bsem=bsem, bbuf=bbuf):
                await_bytes(bbuf.at[k], bsem.at[k])

            if k == CHUNKS - 1:
                pl.when(no_next == 0)(fwd)
            else:
                fwd()
            if k == 0:
                pl.when(no_prev == 0)(bwd)
            else:
                bwd()
    for cp in wcopies:
        cp.wait_send()
    for i in range(3):
        pltpu.make_async_copy(Y[i], O[i], r.lsem.at[len(loads) + i]).wait()


def body(NX, NW, tokens, cotangent, in_weight, conv_weight, out_weight, norm_gain, gate_up_weight, down_weight):
    micro, T, D = tokens.shape
    LW = conv_weight.shape[2]
    HW = gate_up_weight.shape[3]
    HP = -(-HW // 128) * 128
    w_small = jnp.concatenate(
        [norm_gain, jnp.pad(conv_weight[0], ((0, 4), (0, D - LW)))], 0
    )
    GR = D // 128
    L, K = 2, CHUNKS
    vmem = pltpu.VMEM
    dma = pltpu.SemaphoreType.DMA
    n_ag, n_rs = 6 * K, 6 * K
    NY = NZ = next(i for i in range(1, NW + 1) if i * i >= NW)
    plane = (NZ, NY, ROWS, D)
    ins = dict(
        tokens=tokens, cotangent=cotangent, w_in=in_weight[0].transpose(1, 2, 0), w_out=out_weight[0],
        w_gu=gate_up_weight[0].transpose(1, 2, 0), w_dn=down_weight[0], w_small=w_small
    )
    anyspec = pl.BlockSpec(memory_space=pl.ANY)
    vspec = pl.BlockSpec(memory_space=pltpu.VMEM)
    shape = jax.ShapeDtypeStruct
    outs = dict(
        o_layer=(shape((micro, ROWS, D), BF), vspec),
        o_grad=(shape((micro, ROWS, D), F32), vspec),
        o_cv=(shape((4 * LW, D), BF), anyspec),
        o_gu=(shape((2 * HW, D), BF), anyspec),
        o_dn=(shape((HW, D), BF), anyspec),
        o_small=(shape((GR + 8, 128), F32), vspec),
    )
    scratch = dict(
        Cown=vmem((L, 4, LW, D), BF), Cfull=vmem((4, NZ, NY, LW, D), BF),
        Wgu=vmem((L, 2, HP, D), BF), Wdn=vmem((L, HP, D), BF), Wsm=vmem((L, 8, D), F32),
        tok=vmem((K, T, D), BF), cot=vmem((K, T, D), F32), cotb=vmem((K, T, D), BF),
        projB=vmem((K, T, LW), F32), projC=vmem((K, T, LW), F32), projX=vmem((K, T, LW), F32),
        gp=vmem((K, T + 8, LW), F32), conv=vmem((K, T, LW), F32), mixed=vmem((K, T, LW), BF),
        gu=vmem((L, K, T, 2 * HP), F32), hg=vmem((K, T, HP), F32), hid=vmem((L, K, T, HP), BF),
        gub=vmem((L, K, T, 2 * HP), BF), pbf=vmem((K, T, 3 * LW), BF),
        res=vmem((L, K, ROWS, D), F32), rg=vmem((L, K, ROWS, D), F32), g0own=vmem((K, ROWS, D), F32),
        cvg=vmem((K, T + 8, LW), F32),
        norm=vmem((L, K) + plane, BF), u1=vmem((K,) + plane, BF), rb=vmem((L, K) + plane, BF), gbf=vmem((K,) + plane, BF),
        stage=vmem((K, 2) + plane, BF), rva=vmem((n_rs, NY, NZ, ROWS, D // 2), BF), rvb=vmem((n_rs, NZ, NY, ROWS, D // 2), BF),
        rsa=vmem((n_rs, NZ, ROWS, D // 2), BF), rsb=vmem((n_rs, NY, ROWS, D // 2), BF),
        rwa=vmem((n_rs, NZ, ROWS, D // 2), BF), rwb=vmem((n_rs, NY, ROWS, D // 2), BF),
        hs=vmem((K, 16, LW), BF), hb=vmem((K, 16, LW), BF), hgs=vmem((K, 8, LW), F32), hgb=vmem((K, 8, LW), F32),
        proj1=vmem((3, K * ROWS, D), F32), gp1=vmem((K, ROWS + 8, D), F32), conv1=vmem((K, ROWS, D), F32),
        mixed1=vmem((K * ROWS, D), BF), cv1=vmem((K, ROWS + 8, D), F32), pbf1=vmem((K * ROWS, 3 * D), BF),
        h1s=vmem((K, ROWS, D), BF), h1b=vmem((K, ROWS, D), BF), hg1b=vmem((K, 8, D), F32),
        trow=vmem((3, D), F32), tap1g=vmem((3, D), F32), taps1=vmem((NW, 8, 128), F32),
        pms=vmem((NW, K * ROWS, 4 * LW), BF), pm=vmem((NW, K * ROWS, 4 * LW), BF),
        lost=vmem((L, K, ROWS, D), BF), ligst=vmem((L, K, ROWS, D), F32),
        lo=vmem((micro, ROWS, D), BF), ig=vmem((micro, ROWS, D), F32),
        Xgu=vmem((L, 2 * HW, D), BF), Xdn=vmem((L, HW, D), BF), Xcv=vmem((L, 4 * LW, D), BF),
        Ygu=vmem((2 * HW, D), BF), Ydn=vmem((HW, D), BF), Ycv=vmem((4 * LW, D), BF),
        Rgu=vmem((NX, 2 * HW // NX, D), BF), Rdn=vmem((NX, HW, D // NX), BF), Rcv=vmem((NX, 4 * LW // NX, D), BF),
        gacc=vmem((L, 1, D), F32), tacc=vmem((8, 128), F32), gst=vmem((L, NW, GR + 8, 128), F32),
        gex=vmem((L, NW, GR + 8, 128), F32), sm=vmem((L, GR + 8, 128), F32),
        smY=vmem((GR + 8, 128), F32), smR=vmem((NX, GR + 8, 128), F32),
        lsem=dma((16,)), wsend=dma((5,)), wrecv=dma((5,)), ags=dma((n_ag, 4)), agr=dma((n_ag, 4)),
        rss=dma((n_rs, 4)), rsr=dma((n_rs, 4)), hsend=dma((K,)), hrecv=dma((K,)), hgsend=dma((K,)), hgrecv=dma((K,)),
        h1send=dma((K,)), h1recv=dma((K,)), hg1send=dma((K,)), hg1recv=dma((K,)), pmsem=dma((2,)),
        gwsem=dma((11,)), gxs=dma((4,)), gxr=dma((4,)), gcs=dma((4,)), gcr=dma((4,)),
        osend=dma((2, K)), orecv=dma((2, K)), csend=dma((4,)), crecv=dma((4,)), xsend=dma((4,)), xrecv=dma((4,)),
        vsend=dma((3,)), vrecv=dma((3,)), gsend=dma((L,)), grecv=dma((L,)),
    )
    names = tuple(ins) + tuple(outs) + tuple(scratch)
    layer, grad, g_cv, g_gu, g_dn, small = pl.pallas_call(
        functools.partial(kernel, (NX, NW, T, D, LW, HW, HP), names),
        out_shape=tuple(o[0] for o in outs.values()),
        in_specs=[anyspec] * len(ins),
        out_specs=tuple(o[1] for o in outs.values()),
        scratch_shapes=list(scratch.values()),
        compiler_params=pltpu.CompilerParams(
            collective_id=0, has_side_effects=True, vmem_limit_bytes=63 << 20
        ),
    )(*ins.values())
    return (
        layer[None],
        grad[None],
        g_cv[: 3 * LW].reshape(3, LW, D).transpose(2, 0, 1).astype(F32)[None],
        small[GR : GR + 3, :LW][None],
        g_cv[3 * LW :].astype(F32)[None],
        small[:GR].reshape(1, D),
        g_gu.reshape(2, HW, D).transpose(2, 0, 1).astype(F32)[None],
        g_dn.astype(F32)[None],
    )


def solution(mesh):
    in_specs = (
        P(None, "seq", None),
        P(None, "seq", None),
        P("section", None, None, "wa"),
        P("section", None, "wa"),
        P("section", "wa", None),
        P("section", None),
        P("section", None, None, "wa"),
        P("section", "wa", None),
    )
    out_specs = (
        P("section", None, ("seq", "wa"), None),
        P("section", None, ("seq", "wa"), None),
        P("section", None, None, "wa"),
        P("section", None, "wa"),
        P("section", "wa", None),
        P("section", None),
        P("section", None, None, "wa"),
        P("section", "wa", None),
    )
    fn = functools.partial(body, mesh.shape["seq"], mesh.shape["wa"])
    return jax.shard_map(fn, mesh=mesh, in_specs=in_specs, out_specs=out_specs, check_vma=False)
```

time: 2040 us -> 212 us (0.10)
  waiting for transfers between devices: 1610 us -> 0 us
  Pallas kernels: 0 us -> 200 us
  blocking collectives: 197 us -> 0 us
  matrix products: 80.8 us -> 0 us
  other arithmetic: 67.3 us -> 6.73 us
  starting transfers between devices: 32.9 us -> 0 us
  local copies, waits for them, and re-layouts: 28.3 us -> 4.34 us
    psum x11 -> x0, waiting for transfers between devices: 888 us -> none  [the longest x5 427 us: body(): lax.psum(jnp.dot(mixed_in, out_matrix, preferred_element_type=jnp.float32...]
    reduce_scatter x10 -> x0, waiting for transfers between devices: 692 us -> none  [the longest x5 349 us: body(): lax.psum_scatter(contract_last(proj_bf, in_matrix).astype(jnp.bfloat16),...]
    pallas_call x0 -> x1, Pallas kernels: none -> 200 us  [body(): pl.pallas_call(functools.partial(kernel, (NX, NW, T, D, LW, HW, HP), name...]
    all_gather x8 -> x0, blocking collectives: 187 us -> none  [the longest x4 93.4 us: body(): received = lax.all_gather(arrived, 'wa', axis=0, tiled=True)]
    dot_general x60 -> x0, matrix products: 80.8 us -> none  [the longest x20 32.8 us: contract_first(): lax.dot_general(lhs_matrix, rhs_matrix, (((0,), (0,)), ((), ())), preferr...]
    ppermute x18 -> x0, waiting for transfers between devices: 33.8 us -> none  [the longest x10 25 us: passed_along(): return lax.ppermute(block, axis, route)]
    ppermute x18 -> x0, starting transfers between devices: 31.4 us -> none  [the longest x10 21 us: passed_along(): return lax.ppermute(block, axis, route)]
    unnamed x347 -> x14, local copies, waits for them, and re-layouts: 25.4 us -> 2.63 us
  transfers between devices with their start and end apart: 39 -> 0, of which waited for: 38 -> 0; matrix products, arithmetic and copies ran while one was open for 2% -> 0% of each run, Pallas kernels for 0% -> 0%
where the time goes in v1:
time: 212 us
  Pallas kernels  200 us (94%)
  other arithmetic  6.73 us (3%)
  local copies, waits for them, and re-layouts  4.34 us (2%)
    pallas_call x1, Pallas kernels, body(): pl.pallas_call(functools.partial(kernel, (NX, NW, T, D, LW, HW, HP), name...  200 us

profile of v1, /device:TPU:0, one launch (start us, length us, event | category | flops | bytes accessed | tf_op | source)
XLA Modules:
  0.0 211.8 jit_solution(12434790392790945639)
XLA Ops:
  0.6 0.7 copy.19
  1.3 1.3 select_maximum_fusion.refs_6_
  2.6 200.1 %shard_map.143 = (bf16[4,16,1024]{2,1,0:T(8,128)(2,1)}, f32[4,16,1024]{2,1,0:T(8,128)}, bf16[256,1024]{1,0:T(8,128)(2,1)}, bf16[576,1024]{1,0:T(8,128)(2,1)}, bf...) custom-call(bf16[4,256,1024]{2,1,0:T(8,128)(2,1)} %refs_0_.1, f32[4,256,1024]{2,1,0:T(8,128)} %refs_1_.1, ...), custom_call_target="tpu_custom_call" | custom-call | tf_op jit(solution)/shard_map/pallas_call | solution.py:1069
  202.7 0.0 copy-start.4
  202.7 0.0 copy-start
  202.7 1.1 slice.12
  203.9 1.0 convert_bitcast_fusion.1
  204.8 1.6 bitcast_convert_fusion.1
  206.4 0.0 copy-done.4
  206.4 0.6 slice.15
  207.0 0.6 copy.16
  207.6 0.0 copy-done
  207.6 0.0 copy-start.1
  207.6 1.7 convert_bitcast_fusion
  209.3 0.0 copy-start.3
  209.3 0.0 copy-start.2
  209.3 0.0 copy-done.1
  209.3 1.1 bitcast_convert_fusion
  210.5 0.0 copy-done.3
  210.5 0.7 copy.22
  211.1 0.0 copy-done.2
  211.1 0.7 copy.23
  (1 shorter events, 0.0 us)
Async XLA Ops:
  202.7 3.7 %copy-start.4 = (f32[16,128]{1,0:T(8,128)S(1)}, f32[16,128]{1,0:T(8,128)}, u32[]{:S(2)}) copy-start(f32[16,128]{1,0:T(8,128)} %get-tuple-element.17) | copy-start | bytes 24580
  202.7 4.9 %copy-start = (bf16[576,1024]{1,0:T(8,128)(2,1)S(1)}, bf16[576,1024]{1,0:T(8,128)(2,1)}, u32[]{:S(2)}) copy-start(bf16[576,1024]{1,0:T(8,128)(2,1)} %get-tuple-element.18) | copy-start | bytes 3538948
  207.6 1.7 copy-start.1
  209.3 1.1 copy-start.3
  209.3 1.8 copy-start.2

commit v2 on v1

--- a/solution.py
+++ b/solution.py
@@ -696,7 +696,17 @@
     X = [r.Xgu, r.Xdn, r.Xcv]
     Y = [r.Ygu, r.Ydn, r.Ycv]
     R = [r.Rgu, r.Rdn, r.Rcv]
-    O = [r.o_gu, r.o_dn, r.o_cv]
+    flush = [
+        [(r.Ygu, r.o_gu)],
+        [(r.Ydn, r.o_dn)],
+        [(r.Ycv.at[pl.ds(0, 3 * LW)], r.o_in), (r.Ycv.at[pl.ds(3 * LW, LW)], r.o_out)],
+    ]
+
+    def flush_copies(i):
+        return [
+            pltpu.make_async_copy(src, dst, r.lsem.at[len(loads) + i + n]) for n, (src, dst) in enumerate(flush[i])
+        ]
+
     by_row = [True, False, True]
 
     def part(ref, i, q):
@@ -795,7 +805,8 @@
             await_bytes(R[i].at[pl.ds(0, NX - 1)], r.vrecv.at[i])
             await_bytes(R[i].at[pl.ds(0, NX - 1)], r.xsend.at[i])
             await_bytes(R[i].at[pl.ds(0, NX - 1)], r.vsend.at[i])
-            pltpu.make_async_copy(Y[i], O[i], r.lsem.at[len(loads) + i]).start()
+            for cp in flush_copies(i):
+                cp.start()
 
         @pl.when(c != l)
         def _():
@@ -854,7 +865,9 @@
             total = r.smR[0]
             for j in range(1, NX):
                 total = total + r.smR[j]
-            r.o_small[...] = total
+            for i in range(GR):
+                r.o_gain[:, i * 128 : (i + 1) * 128] = total[i : i + 1]
+            r.o_tap[...] = total[GR : GR + 3, :LW]
             await_bytes(r.smR.at[pl.ds(0, NX - 1)], r.xsend.at[3])
 
         @pl.when(c != l)
@@ -921,39 +934,41 @@
     mids("ag", 1, "r", BA)
     gain_recv(1)
     small_send(1)
+    x_gather(1, 0)
+    x_gather(1, 1)
+    x_reduce(0, 0)
+    x_reduce(0, 1)
     t2(0, B)
     t2(0, A)
-    x_reduce(0, 0)
-    x_reduce(0, 1)
     mids("ag", 0, "r", BA)
     gain_send(0)
     w2_1()
     core_send(1, 2)
     t3(0, B)
     t3(0, A)
-    x_gather(1, 0)
-    x_gather(1, 1)
+    x_reduce(1, 2)
+    small_x(1)
+    x_gather(0, 0)
+    x_gather(0, 1)
     t4(0, B)
     t4(0, A)
     w2_0()
     core_send(0, 2)
     mids("rs", 0, "d", BA)
-    x_gather(0, 0)
-    x_gather(0, 1)
-    x_reduce(1, 2)
-    small_x(1)
+    x_reduce(0, 2)
     gain_recv(0)
     small_send(0)
-    x_reduce(0, 2)
     small_x(0)
+    x_gather(1, 2)
     t5(0, B)
     t5(0, A)
-    x_gather(1, 2)
+    for i in range(3):
+        x_finish(1, i)
     x_gather(0, 2)
-    for l in (1, 0):
-        for i in range(3):
-            x_finish(l, i)
-        small_finish(l)
+    small_finish(1)
+    for i in range(3):
+        x_finish(0, i)
+    small_finish(0)
     gather_close()
     await_bytes(r.pm.at[pl.ds(0, NW - 1)], r.pmsem.at[0])
 
@@ -997,7 +1012,8 @@
     for cp in wcopies:
         cp.wait_send()
     for i in range(3):
-        pltpu.make_async_copy(Y[i], O[i], r.lsem.at[len(loads) + i]).wait()
+        for cp in flush_copies(i):
+            cp.wait()
 
 
 def body(NX, NW, tokens, cotangent, in_weight, conv_weight, out_weight, norm_gain, gate_up_weight, down_weight):
@@ -1025,10 +1041,12 @@
     outs = dict(
         o_layer=(shape((micro, ROWS, D), BF), vspec),
         o_grad=(shape((micro, ROWS, D), F32), vspec),
-        o_cv=(shape((4 * LW, D), BF), anyspec),
+        o_in=(shape((3 * LW, D), BF), anyspec),
+        o_out=(shape((LW, D), BF), anyspec),
         o_gu=(shape((2 * HW, D), BF), anyspec),
         o_dn=(shape((HW, D), BF), anyspec),
-        o_small=(shape((GR + 8, 128), F32), vspec),
+        o_gain=(shape((1, D), F32), vspec),
+        o_tap=(shape((3, LW), F32), vspec),
     )
     scratch = dict(
         Cown=vmem((L, 4, LW, D), BF), Cfull=vmem((4, NZ, NY, LW, D), BF),
@@ -1066,7 +1084,7 @@
         vsend=dma((3,)), vrecv=dma((3,)), gsend=dma((L,)), grecv=dma((L,)),
     )
     names = tuple(ins) + tuple(outs) + tuple(scratch)
-    layer, grad, g_cv, g_gu, g_dn, small = pl.pallas_call(
+    layer, grad, g_in, g_out, g_gu, g_dn, g_gain, g_tap = pl.pallas_call(
         functools.partial(kernel, (NX, NW, T, D, LW, HW, HP), names),
         out_shape=tuple(o[0] for o in outs.values()),
         in_specs=[anyspec] * len(ins),
@@ -1079,10 +1097,10 @@
     return (
         layer[None],
         grad[None],
-        g_cv[: 3 * LW].reshape(3, LW, D).transpose(2, 0, 1).astype(F32)[None],
-        small[GR : GR + 3, :LW][None],
-        g_cv[3 * LW :].astype(F32)[None],
-        small[:GR].reshape(1, D),
+        g_in.reshape(3, LW, D).transpose(2, 0, 1).astype(F32)[None],
+        g_tap[None],
+        g_out.astype(F32)[None],
+        g_gain,
         g_gu.reshape(2, HW, D).transpose(2, 0, 1).astype(F32)[None],
         g_dn.astype(F32)[None],
     )

time: 212 us -> 202 us (0.953)
  Pallas kernels: 200 us -> 190 us
    pallas_call x1, Pallas kernels: 200 us -> 190 us  [body(): pl.pallas_call(functools.partial(kernel, (NX, NW, T, D, LW, HW, HP), name...]
where the time goes in v2:
time: 202 us
  Pallas kernels  190 us (94%)
  other arithmetic  7.15 us (4%)
  local copies, waits for them, and re-layouts  3.22 us (2%)
    pallas_call x1, Pallas kernels, body(): pl.pallas_call(functools.partial(kernel, (NX, NW, T, D, LW, HW, HP), name...  190 us

profile of v2, /device:TPU:0, one launch (start us, length us, event | category | flops | bytes accessed | tf_op | source)
XLA Modules:
  0.0 201.5 jit_solution(12112545823325852126)
XLA Ops:
  0.6 0.7 copy.19
  1.3 1.3 select_maximum_fusion.refs_6_
  2.6 190.5 %shard_map.143 = (bf16[4,16,1024]{2,1,0:T(8,128)(2,1)}, f32[4,16,1024]{2,1,0:T(8,128)}, bf16[192,1024]{1,0:T(8,128)(2,1)}, bf16[64,1024]{1,0:T(8,128)(2,1)}, bf1...) custom-call(bf16[4,256,1024]{2,1,0:T(8,128)(2,1)} %refs_0_.1, ...), custom_call_target="tpu_custom_call" | custom-call | tf_op jit(solution)/shard_map/pallas_call | solution.py:1087
  193.1 0.0 copy-start
  193.1 3.0 %convert_bitcast_fusion = f32[1,1024,2,288]{1,3,2,0:T(8,128)} fusion(bf16[2,288,1024]{2,1,0:T(8,128)(2,1)} %bitcast.32), kind=kLoop, calls=%fused_computation | loop fusion | flops 589824 | bytes 3538944 | tf_op jit(solution)/shard_map/broadcast_in_dim | solution.py:1104
  196.1 0.0 copy-start.1
  196.1 0.0 copy-done
  196.1 0.0 copy-start.3
  196.1 1.1 bitcast_convert_fusion
  197.3 0.0 copy-start.6
  197.3 0.0 copy-start.4
  197.3 0.0 copy-start.2
  197.3 0.0 copy-done.1
  197.3 0.0 copy-start.5
  197.3 1.0 convert_bitcast_fusion.1
  198.3 0.0 copy-done.3
  198.3 0.7 bitcast_convert_fusion.1
  199.0 0.0 copy-done.6
  199.0 0.6 copy.16
  199.5 0.0 copy-done.4
  199.6 0.7 copy.23
  200.2 0.0 copy-done.2
  200.2 0.7 copy.24
  200.9 0.0 copy-done.5
  200.9 0.6 copy.25
Async XLA Ops:
  193.1 3.0 %copy-start = (bf16[288,1024]{1,0:T(8,128)(2,1)S(1)}, bf16[288,1024]{1,0:T(8,128)(2,1)}, u32[]{:S(2)}) copy-start(bf16[288,1024]{1,0:T(8,128)(2,1)} %get-tuple-element.23) | copy-start | bytes 1769476
  196.1 1.2 copy-start.1
  196.1 2.1 %copy-start.3 = (bf16[64,1024]{1,0:T(8,128)(2,1)S(1)}, bf16[64,1024]{1,0:T(8,128)(2,1)}, u32[]{:S(2)}) copy-start(bf16[64,1024]{1,0:T(8,128)(2,1)} %get-tuple-element.20) | copy-start | bytes 393220
  197.3 1.7 copy-start.6
  197.3 2.3 %copy-start.4 = (bf16[4,16,1024]{2,1,0:T(8,128)(2,1)S(1)}, bf16[4,16,1024]{2,1,0:T(8,128)(2,1)}, u32[]{:S(2)}) copy-start(bf16[4,16,1024]{2,1,0:T(8,128)(2,1)} %get-tuple-element.16) | copy-start | bytes 393220
  197.3 2.9 %copy-start.2 = (f32[4,16,1024]{2,1,0:T(8,128)S(1)}, f32[4,16,1024]{2,1,0:T(8,128)}, u32[]{:S(2)}) copy-start(f32[4,16,1024]{2,1,0:T(8,128)} %get-tuple-element.17) | copy-start | bytes 786436
  197.3 3.6 %copy-start.5 = (f32[1,1024]{1,0:T(1,128)S(1)}, f32[1,1024]{1,0:T(1,128)}, u32[]{:S(2)}) copy-start(f32[1,1024]{1,0:T(1,128)} %get-tuple-element.45) | copy-start | bytes 12292

commit v3 on v2

--- a/solution.py
+++ b/solution.py
@@ -101,16 +101,21 @@
 
     wpairs = [
         (r.w_in, r.Cown.at[c, pl.ds(0, 3)]),
-        (r.w_small, r.Wsm.at[c]),
+        (r.Wsm.at[c], r.Wsm.at[c]),
         (r.w_gu, r.Wgu.at[c, :, pl.ds(0, HW)]),
         (r.w_dn, r.Wdn.at[c, pl.ds(0, HW)]),
         (r.w_out, r.Cown.at[c, 3]),
     ]
     l_tok = [load(r.tokens.at[c], r.tok.at[0]), None]
-    l_w = [load(*wpairs[0]), load(*wpairs[1])]
+    l_w = [load(*wpairs[0]), None]
     l_tok[1] = load(r.tokens.at[2 + c], r.tok.at[1])
     l_w += [load(*p) for p in wpairs[2:]]
     l_cot = [load(r.cotangent.at[2 * k + c], r.cot.at[k]) for k in range(CHUNKS)]
+
+    r.Wsm[c] = jnp.zeros((8, D), F32)
+    r.Wsm[c, 0:1] = r.w_gain[...]
+    for j in range(3):
+        r.Wsm[c, j + 1 : j + 2, :LW] = r.w_conv[j]
 
     bar = pltpu.get_barrier_semaphore()
 
@@ -148,7 +153,8 @@
     def need_w(i):
         if i not in wready:
             wready.add(i)
-            loads[l_w[i]].wait()
+            if l_w[i] is not None:
+                loads[l_w[i]].wait()
             wcopies[i].wait_recv()
 
     full = r.Cfull
@@ -415,6 +421,8 @@
             r.hid[l, k, rows] = (gate * jax.nn.sigmoid(gate) * up).astype(BF)
 
         row_loop(T, 32, act)
+
+    def s4_down(l, k):
         st = stage_get(k)
         for n0, n in tiles(D):
             put(st, n0, n, dot_nn(r.hid[l, k], r.Wdn[l, :, n0 : n0 + n]))
@@ -889,7 +897,9 @@
     gather_x(1)
     mids("ag", 0, "n", AB)
     s4(0, A)
+    s4_down(0, A)
     s4(0, B)
+    s4_down(0, B)
     gather_x(2)
     prep_cot(A)
     mids("rs", 0, "b", AB)
@@ -907,21 +917,21 @@
     s4(1, A)
     s4(1, B)
     t1(1, B)
-    mids("rs", 1, "b", AB)
     t1(1, A)
-    mids("ag", 1, "u", AB)
     mids("rs", 1, "c", BA)
     w1(1)
     t2(1, B)
     t2(1, A)
+    mids("ag", 1, "u", AB)
     b1a()
+    s4_down(1, A)
+    s4_down(1, B)
     core_send(1, 0)
     core_send(1, 1)
     b1b()
-    s5(1, A)
-    s5(1, B)
     mids("ag", 0, "g", BA)
     gain_send(1)
+    mids("rs", 1, "b", AB)
     b1_exchange()
     x_reduce(1, 0)
     x_reduce(1, 1)
@@ -930,6 +940,8 @@
     w1(0)
     core_send(0, 0)
     core_send(0, 1)
+    s5(1, A)
+    s5(1, B)
     mids("rs", 0, "c", BA)
     mids("ag", 1, "r", BA)
     gain_recv(1)
@@ -1021,9 +1033,6 @@
     LW = conv_weight.shape[2]
     HW = gate_up_weight.shape[3]
     HP = -(-HW // 128) * 128
-    w_small = jnp.concatenate(
-        [norm_gain, jnp.pad(conv_weight[0], ((0, 4), (0, D - LW)))], 0
-    )
     GR = D // 128
     L, K = 2, CHUNKS
     vmem = pltpu.VMEM
@@ -1033,7 +1042,8 @@
     plane = (NZ, NY, ROWS, D)
     ins = dict(
         tokens=tokens, cotangent=cotangent, w_in=in_weight[0].transpose(1, 2, 0), w_out=out_weight[0],
-        w_gu=gate_up_weight[0].transpose(1, 2, 0), w_dn=down_weight[0], w_small=w_small
+        w_gu=gate_up_weight[0].transpose(1, 2, 0), w_dn=down_weight[0],
+        w_gain=norm_gain, w_conv=conv_weight.transpose(1, 0, 2)
     )
     anyspec = pl.BlockSpec(memory_space=pl.ANY)
     vspec = pl.BlockSpec(memory_space=pltpu.VMEM)
@@ -1087,7 +1097,7 @@
     layer, grad, g_in, g_out, g_gu, g_dn, g_gain, g_tap = pl.pallas_call(
         functools.partial(kernel, (NX, NW, T, D, LW, HW, HP), names),
         out_shape=tuple(o[0] for o in outs.values()),
-        in_specs=[anyspec] * len(ins),
+        in_specs=[anyspec] * (len(ins) - 2) + [vspec] * 2,
         out_specs=tuple(o[1] for o in outs.values()),
         scratch_shapes=list(scratch.values()),
         compiler_params=pltpu.CompilerParams(

time: 202 us -> 197 us (0.975)
    pallas_call x1, Pallas kernels: 190 us -> 188 us  [body(): pl.pallas_call(functools.partial(kernel, (NX, NW, T, D, LW, HW, HP), name...]
where the time goes in v3:
time: 197 us
  Pallas kernels  188 us (95%)
  other arithmetic  5.85 us (3%)
  local copies, waits for them, and re-layouts  2.54 us (1%)
    pallas_call x1, Pallas kernels, body(): pl.pallas_call(functools.partial(kernel, (NX, NW, T, D, LW, HW, HP), name...  188 us

profile of v3, /device:TPU:0, one launch (start us, length us, event | category | flops | bytes accessed | tf_op | source)
XLA Modules:
  0.0 197.1 jit_solution(4932149324952343676)
XLA Ops:
  0.6 188.1 %shard_map.143 = (bf16[4,16,1024]{2,1,0:T(8,128)(2,1)}, f32[4,16,1024]{2,1,0:T(8,128)}, bf16[192,1024]{1,0:T(8,128)(2,1)}, bf16[64,1024]{1,0:T(8,128)(2,1)}, bf1...) custom-call(bf16[4,256,1024]{2,1,0:T(8,128)(2,1)} %refs_0_.1, ...), custom_call_target="tpu_custom_call" | custom-call | tf_op jit(solution)/shard_map/pallas_call | solution.py:1097
  188.7 0.0 copy-start
  188.7 3.0 %convert_bitcast_fusion = f32[1,1024,2,288]{1,3,2,0:T(8,128)} fusion(bf16[2,288,1024]{2,1,0:T(8,128)(2,1)} %bitcast.30), kind=kLoop, calls=%fused_computation | loop fusion | flops 589824 | bytes 3538944 | tf_op jit(solution)/shard_map/broadcast_in_dim | solution.py:1114
  191.7 0.0 copy-start.1
  191.7 0.0 copy-done
  191.8 0.0 copy-start.3
  191.8 1.1 bitcast_convert_fusion
  192.9 0.0 copy-start.6
  192.9 0.0 copy-start.4
  192.9 0.0 copy-start.2
  192.9 0.0 copy-done.1
  192.9 0.0 copy-start.5
  192.9 1.0 convert_bitcast_fusion.1
  193.9 0.0 copy-done.3
  193.9 0.7 bitcast_convert_fusion.1
  194.6 0.0 copy-done.6
  194.6 0.6 copy.16
  195.2 0.0 copy-done.4
  195.2 0.7 copy.20
  195.8 0.0 copy-done.2
  195.8 0.7 copy.21
  196.5 0.0 copy-done.5
  196.5 0.6 copy.22
Async XLA Ops:
  188.7 3.0 %copy-start = (bf16[288,1024]{1,0:T(8,128)(2,1)S(1)}, bf16[288,1024]{1,0:T(8,128)(2,1)}, u32[]{:S(2)}) copy-start(bf16[288,1024]{1,0:T(8,128)(2,1)} %get-tuple-element.23) | copy-start | bytes 1769476
  191.7 1.2 copy-start.1
  191.8 2.1 %copy-start.3 = (bf16[64,1024]{1,0:T(8,128)(2,1)S(1)}, bf16[64,1024]{1,0:T(8,128)(2,1)}, u32[]{:S(2)}) copy-start(bf16[64,1024]{1,0:T(8,128)(2,1)} %get-tuple-element.20) | copy-start | bytes 393220
  192.9 1.7 copy-start.6
  192.9 2.3 %copy-start.4 = (bf16[4,16,1024]{2,1,0:T(8,128)(2,1)S(1)}, bf16[4,16,1024]{2,1,0:T(8,128)(2,1)}, u32[]{:S(2)}) copy-start(bf16[4,16,1024]{2,1,0:T(8,128)(2,1)} %get-tuple-element.16) | copy-start | bytes 393220
  192.9 2.9 %copy-start.2 = (f32[4,16,1024]{2,1,0:T(8,128)S(1)}, f32[4,16,1024]{2,1,0:T(8,128)}, u32[]{:S(2)}) copy-start(f32[4,16,1024]{2,1,0:T(8,128)} %get-tuple-element.17) | copy-start | bytes 786436
  192.9 3.6 %copy-start.5 = (f32[1,1024]{1,0:T(1,128)S(1)}, f32[1,1024]{1,0:T(1,128)}, u32[]{:S(2)}) copy-start(f32[1,1024]{1,0:T(1,128)} %get-tuple-element.45) | copy-start | bytes 12292

commit v4 on v3

--- a/solution.py
+++ b/solution.py
@@ -943,7 +943,6 @@
     s5(1, A)
     s5(1, B)
     mids("rs", 0, "c", BA)
-    mids("ag", 1, "r", BA)
     gain_recv(1)
     small_send(1)
     x_gather(1, 0)
@@ -954,26 +953,27 @@
     t2(0, A)
     mids("ag", 0, "r", BA)
     gain_send(0)
-    w2_1()
-    core_send(1, 2)
     t3(0, B)
     t3(0, A)
-    x_reduce(1, 2)
-    small_x(1)
+    mids("ag", 1, "r", BA)
     x_gather(0, 0)
     x_gather(0, 1)
     t4(0, B)
     t4(0, A)
     w2_0()
     core_send(0, 2)
+    w2_1()
+    core_send(1, 2)
     mids("rs", 0, "d", BA)
     x_reduce(0, 2)
     gain_recv(0)
     small_send(0)
     small_x(0)
-    x_gather(1, 2)
+    x_reduce(1, 2)
+    small_x(1)
     t5(0, B)
     t5(0, A)
+    x_gather(1, 2)
     for i in range(3):
         x_finish(1, i)
     x_gather(0, 2)

time: 197 us -> 195 us (0.990)
  Pallas kernels: 188 us -> 186 us
    pallas_call x1, Pallas kernels: 188 us -> 186 us  [body(): pl.pallas_call(functools.partial(kernel, (NX, NW, T, D, LW, HW, HP), name...]
where the time goes in v4:
time: 195 us
  Pallas kernels  186 us (95%)
  other arithmetic  5.85 us (3%)
  local copies, waits for them, and re-layouts  2.54 us (1%)
    pallas_call x1, Pallas kernels, body(): pl.pallas_call(functools.partial(kernel, (NX, NW, T, D, LW, HW, HP), name...  186 us

profile of v4, /device:TPU:0, one launch (start us, length us, event | category | flops | bytes accessed | tf_op | source)
XLA Modules:
  0.0 194.8 jit_solution(12305180845204129318)
XLA Ops:
  0.6 185.8 %shard_map.143 = (bf16[4,16,1024]{2,1,0:T(8,128)(2,1)}, f32[4,16,1024]{2,1,0:T(8,128)}, bf16[192,1024]{1,0:T(8,128)(2,1)}, bf16[64,1024]{1,0:T(8,128)(2,1)}, bf1...) custom-call(bf16[4,256,1024]{2,1,0:T(8,128)(2,1)} %refs_0_.1, ...), custom_call_target="tpu_custom_call" | custom-call | tf_op jit(solution)/shard_map/pallas_call | solution.py:1097
  186.4 0.0 copy-start
  186.4 3.0 %convert_bitcast_fusion = f32[1,1024,2,288]{1,3,2,0:T(8,128)} fusion(bf16[2,288,1024]{2,1,0:T(8,128)(2,1)} %bitcast.30), kind=kLoop, calls=%fused_computation | loop fusion | flops 589824 | bytes 3538944 | tf_op jit(solution)/shard_map/broadcast_in_dim | solution.py:1114
  189.5 0.0 copy-start.1
  189.5 0.0 copy-done
  189.5 0.0 copy-start.3
  189.5 1.1 bitcast_convert_fusion
  190.6 0.0 copy-start.6
  190.6 0.0 copy-start.4
  190.6 0.0 copy-start.2
  190.6 0.0 copy-done.1
  190.6 0.0 copy-start.5
  190.6 1.0 convert_bitcast_fusion.1
  191.6 0.0 copy-done.3
  191.6 0.7 bitcast_convert_fusion.1
  192.3 0.0 copy-done.6
  192.3 0.6 copy.16
  192.9 0.0 copy-done.4
  192.9 0.7 copy.20
  193.5 0.0 copy-done.2
  193.5 0.7 copy.21
  194.2 0.0 copy-done.5
  194.2 0.6 copy.22
Async XLA Ops:
  186.4 3.0 %copy-start = (bf16[288,1024]{1,0:T(8,128)(2,1)S(1)}, bf16[288,1024]{1,0:T(8,128)(2,1)}, u32[]{:S(2)}) copy-start(bf16[288,1024]{1,0:T(8,128)(2,1)} %get-tuple-element.23) | copy-start | bytes 1769476
  189.5 1.2 copy-start.1
  189.5 2.1 %copy-start.3 = (bf16[64,1024]{1,0:T(8,128)(2,1)S(1)}, bf16[64,1024]{1,0:T(8,128)(2,1)}, u32[]{:S(2)}) copy-start(bf16[64,1024]{1,0:T(8,128)(2,1)} %get-tuple-element.20) | copy-start | bytes 393220
  190.6 1.7 copy-start.6
  190.6 2.3 %copy-start.4 = (bf16[4,16,1024]{2,1,0:T(8,128)(2,1)S(1)}, bf16[4,16,1024]{2,1,0:T(8,128)(2,1)}, u32[]{:S(2)}) copy-start(bf16[4,16,1024]{2,1,0:T(8,128)(2,1)} %get-tuple-element.16) | copy-start | bytes 393220
  190.6 2.9 %copy-start.2 = (f32[4,16,1024]{2,1,0:T(8,128)S(1)}, f32[4,16,1024]{2,1,0:T(8,128)}, u32[]{:S(2)}) copy-start(f32[4,16,1024]{2,1,0:T(8,128)} %get-tuple-element.17) | copy-start | bytes 786436
  190.6 3.6 %copy-start.5 = (f32[1,1024]{1,0:T(1,128)S(1)}, f32[1,1024]{1,0:T(1,128)}, u32[]{:S(2)}) copy-start(f32[1,1024]{1,0:T(1,128)} %get-tuple-element.45) | copy-start | bytes 12292
